TPU v7x, 512 devices: a whole 4x8x8 slice. The times are simulated.
512 devices in a mesh: ia: 4 (over x), ja: 16 (over z, core), ka: 8 (over y).
Axes of the slice: x: 4, y: 8, z: 8, core: 2. Of those that a mesh axis runs over, the one named last changes fastest.
Arguments:
- tensor: bfloat16 [512, 512, 1024], P('ia', 'ja', 'ka'), may hold values from -21000 to 21000
- factor_b: float32 [16, 32, 32], P('ja', ('ia', 'ka')), may hold values from -6 to 6
- factor_c: float32 [8, 128, 32], P('ka', ('ia', 'ja')), may hold values from -6 to 6
Outputs:
- factor_a_out: float32 [4, 128, 32], P('ia', ('ja', 'ka'))
- factor_b_out: float32 [16, 32, 32], P('ja', ('ia', 'ka'))
- factor_c_out: float32 [8, 128, 32], P('ka', ('ia', 'ja'))
All inputs are finite; a program needn't handle non-finite values.
Results may differ from a plain program's by a relative error of at most 0.0041.
Values may be sent and summed in bfloat16 or wider, within the bound.
No kernel may reach another device: no remote copies, remote signals or barrier semaphores. Data moves between devices by JAX's collectives and lax.ppermute only.
A program may use at most 64 MiB of HBM per device.

v0:
```python
import jax
import jax.numpy as jnp
from jax import lax
from jax.sharding import PartitionSpec as P

HIGH = lax.Precision.HIGHEST


def gram_of(matrix):
    return jnp.dot(matrix.T, matrix, precision=HIGH)


def solve_rows(summed, vmatrix):
    lower_factor = jnp.linalg.cholesky(vmatrix)
    forward = lax.linalg.triangular_solve(lower_factor, summed.T, left_side=True, lower=True)
    backward = lax.linalg.triangular_solve(
        lower_factor, forward, left_side=True, lower=True, transpose_a=True
    )
    return backward.T


def rescale(solved, gram_raw, total):
    factor_scale = lax.rsqrt(jnp.diagonal(gram_raw) / total + 1e-06)
    return (
        solved * factor_scale[None, :],
        gram_raw * factor_scale[:, None] * factor_scale[None, :],
    )


def owner_update(summed, vmatrix, total):
    solved = solve_rows(summed, vmatrix)
    gram_raw = lax.psum(gram_of(solved), ("ia", "ja", "ka"))
    return rescale(solved, gram_raw, total)


def collect_a(owned_a):
    return lax.all_gather(owned_a, ("ja", "ka"), axis=0, tiled=True)


def collect_b(owned_b):
    return lax.all_gather(owned_b, ("ia", "ka"), axis=0, tiled=True)


def collect_c(owned_c):
    return lax.all_gather(owned_c.astype(jnp.bfloat16), ("ia", "ja"), axis=0, tiled=True)


def local(tensor, factor_b, factor_c):
    rows_i, rows_j, rows_k = tensor.shape
    columns = factor_b.shape[2]
    total_i = rows_i * lax.axis_size("ia")
    total_j = rows_j * lax.axis_size("ja")
    total_k = rows_k * lax.axis_size("ka")
    share_a = rows_i // (lax.axis_size("ja") * lax.axis_size("ka"))
    share_b = rows_j // (lax.axis_size("ia") * lax.axis_size("ka"))
    share_c = rows_k // (lax.axis_size("ia") * lax.axis_size("ja"))
    owned_b = factor_b[0]
    owned_c = factor_c[0]
    gram_b, gram_c = lax.psum((gram_of(owned_b), gram_of(owned_c)), ("ia", "ja", "ka"))
    block_b = collect_b(owned_b)
    block_c = collect_c(owned_c)
    flat_ij = tensor.reshape(rows_i * rows_j, rows_k)
    flat_jk = tensor.reshape(rows_i, rows_j * rows_k)
    product = lax.dot_general(
        block_c, flat_ij, (((0,), (1,)), ((), ())), preferred_element_type=jnp.float32
    )
    along_k = product.reshape(columns, rows_i, rows_j)

    def terms_a(offset, length, along_k=along_k, block_b=block_b):
        return jnp.einsum("rij,jr->ir", along_k, block_b, precision=HIGH)

    summed = lax.psum_scatter(
        terms_a(jnp.int32(0), share_a * lax.axis_size(("ja", "ka"))),
        ("ja", "ka"),
        scatter_dimension=0,
        tiled=True,
    )
    owned_a, gram_a = owner_update(summed, gram_b * gram_c, total_i)
    block_a = collect_a(owned_a)
    reused = along_k

    def terms_b(offset, length, reused=reused, block_a=block_a):
        return jnp.einsum("rij,ir->jr", reused, block_a, precision=HIGH)

    summed = lax.psum_scatter(
        terms_b(jnp.int32(0), share_b * lax.axis_size(("ia", "ka"))),
        ("ia", "ka"),
        scatter_dimension=0,
        tiled=True,
    )
    owned_b, gram_b = owner_update(summed, gram_a * gram_c, total_j)
    block_b = collect_b(owned_b)
    product = lax.dot_general(
        block_a.astype(jnp.bfloat16),
        flat_jk,
        (((0,), (0,)), ((), ())),
        preferred_element_type=jnp.float32,
    )
    along_i = product.reshape(columns, rows_j, rows_k)

    def terms_c(offset, length, along_i=along_i, block_b=block_b):
        return jnp.einsum("rjk,jr->kr", along_i, block_b, precision=HIGH)

    summed = lax.psum_scatter(
        terms_c(jnp.int32(0), share_c * lax.axis_size(("ia", "ja"))),
        ("ia", "ja"),
        scatter_dimension=0,
        tiled=True,
    )
    owned_c, gram_c = owner_update(summed, gram_a * gram_b, total_k)
    return (owned_a[None], owned_b[None], owned_c[None])


def solution(mesh):
    placed = (P("ia", "ja", "ka"), P("ja", ("ia", "ka"), None), P("ka", ("ia", "ja"), None))
    return jax.shard_map(
        local,
        mesh=mesh,
        in_specs=placed,
        out_specs=(
            P("ia", ("ja", "ka"), None),
            P("ja", ("ia", "ka"), None),
            P("ka", ("ia", "ja"), None),
        ),
        check_vma=False,
    )
```

profile of v0, /device:TPU:1, one launch (start us, length us, event | category | flops | bytes accessed | tf_op | source)
XLA Modules:
  0.0 1474.7 jit_solution(17384351041067847836)
XLA Ops:
  0.6 1.3 dynamic-slice.4
  2.6 1.3 dynamic-slice.2
  3.8 1.3 dynamic-slice
  5.1 0.0 copy-start.2
  5.1 0.7 copy-done.2
  5.8 0.0 copy-start.1
  5.8 0.6 copy-done.1
  6.4 0.1 broadcast_multiply_fusion.2
  6.5 29.7 %all-gather = f32[32,1,32]{2,1,0:T(1,128)S(1)} all-gather(f32[1,1,32]{2,1,0:T(1,128)S(1)} %copy-done.1), channel_id=2, replica_groups=mesh['ia'=4,'ja'=16,'ka'=8] {'ia','ka'}, dimensions={0}, use_global_device_ids=true | all-gather | bytes 4224 | tf_op jit(solution)/shard_map/all_gather | solution.py:41
  36.2 0.2 fusion.28
  36.4 108.7 %all-reduce.3 = (f32[32,32]{0,1:T(8,128)S(1)}, f32[32,32]{0,1:T(8,128)S(1)}) all-reduce(f32[32,32]{0,1:T(8,128)S(1)} %broadcast_multiply_fusion.2, f32[32,32]{0,1:T(8,128)S(1)} %fusion.28), channel_id=1, replica_groups=mesh['ia'=4,'ja'=16,'ka'=8] {'ia','ja','ka'}, use_global_device_ids=true, to_apply=%region_0.0 | all-reduce | flops 2048 | bytes 16384 | tf_op jit(solution)/shard_map/psum | solution.py:59
  145.1 0.1 copy.19
  145.2 2.9 cholesky.59
  148.1 0.6 compare_reduce_fusion.2
  148.7 0.7 fusion.6
  149.4 2.4 custom-call.23
  151.8 38.5 %all-gather.1 = bf16[64,2,32]{2,1,0:T(2,128)(2,1)S(1)} all-gather(bf16[1,2,32]{2,1,0:T(2,128)(2,1)S(1)} %fusion.30), channel_id=1, replica_groups=mesh['ia'=4,'ja'=16,'ka'=8] {'ia','ja'}, dimensions={0}, use_global_device_ids=true | all-gather | bytes 8320 | tf_op jit(solution)/shard_map/all_gather | solution.py:45
  190.4 1.7 multiply_reduce_fusion
  192.1 0.1 copy.34
  192.2 484.6 %all-reduce = f32[128,32]{1,0:T(8,128)S(1)} all-reduce(f32[128,32]{1,0:T(8,128)S(1)} %bitcast.154), channel_id=3, replica_groups=mesh['ia'=4,'ja'=16,'ka'=8] {'ja','ka'}, use_global_device_ids=true, to_apply=%region_4.6.clone | all-reduce | flops 4096 | bytes 32768
  676.8 0.8 convolution_bitcast_fusion.1
  677.6 0.1 fusion.20
  677.7 0.1 broadcast_multiply_fusion.1
  677.8 100.6 %psum.37 = f32[32,32]{0,1:T(8,128)S(1)} all-reduce(f32[32,32]{0,1:T(8,128)S(1)} %broadcast_multiply_fusion.1), channel_id=1, replica_groups=mesh['ia'=4,'ja'=16,'ka'=8] {'ia','ja','ka'}, use_global_device_ids=true, to_apply=%region_5.9 | all-reduce | flops 1024 | bytes 8192 | tf_op jit(solution)/shard_map/psum | solution.py:32
  778.4 0.7 gather_fusion
  779.1 0.0 copy-start
  779.1 0.1 fusion.23
  779.2 0.5 bitcast_multiply_fusion.1
  779.7 0.1 copy.22
  779.8 2.9 cholesky.70
  782.7 0.6 compare_reduce_fusion.1
  783.4 0.7 fusion.7
  784.0 2.4 custom-call.25
  786.5 65.1 %all-gather.2 = f32[128,1,32]{2,1,0:T(1,128)S(1)} all-gather(f32[1,1,32]{2,1,0:T(1,128)S(1)} %fusion.36), channel_id=1, replica_groups=mesh['ia'=4,'ja'=16,'ka'=8] {'ja','ka'}, dimensions={0}, use_global_device_ids=true | all-gather | bytes 16512 | tf_op jit(solution)/shard_map/all_gather | solution.py:37
  851.5 0.1 copy.23
  851.6 1.2 fusion.4
  852.7 0.1 copy.37
  852.8 115.0 %all-reduce.1 = f32[32,32]{1,0:T(8,128)S(1)} all-reduce(f32[32,32]{1,0:T(8,128)S(1)} %bitcast.159), channel_id=4, replica_groups=mesh['ia'=4,'ja'=16,'ka'=8] {'ia','ka'}, use_global_device_ids=true, to_apply=%region_6.10.clone | all-reduce | flops 1024 | bytes 8192
  967.8 0.8 convolution_bitcast_fusion
  968.5 0.1 fusion.16
  968.7 0.1 broadcast_multiply_fusion
  968.7 119.2 %psum.38 = f32[32,32]{0,1:T(8,128)S(1)} all-reduce(f32[32,32]{0,1:T(8,128)S(1)} %broadcast_multiply_fusion), channel_id=1, replica_groups=mesh['ia'=4,'ja'=16,'ka'=8] {'ia','ja','ka'}, use_global_device_ids=true, to_apply=%region_7.11 | all-reduce | flops 1024 | bytes 8192 | tf_op jit(solution)/shard_map/psum | solution.py:32
  1088.0 0.7 gather_fusion.1
  1088.7 0.5 bitcast_multiply_fusion
  1089.2 0.1 multiply_multiply_fusion
  1089.3 25.8 %all-gather.3 = f32[32,1,32]{2,1,0:T(1,128)S(1)} all-gather(f32[1,1,32]{2,1,0:T(1,128)S(1)} %fusion.35), channel_id=1, replica_groups=mesh['ia'=4,'ja'=16,'ka'=8] {'ia','ka'}, dimensions={0}, use_global_device_ids=true | all-gather | bytes 4224 | tf_op jit(solution)/shard_map/all_gather | solution.py:41
  1115.2 0.1 copy.38
  1115.2 0.1 copy.24
  1115.3 2.9 cholesky.81
  1118.3 0.6 compare_reduce_fusion
  1118.9 0.7 fusion.8
  1119.6 2.4 custom-call.13
  1122.0 0.0 copy-done
  1122.0 0.5 copy.54
  1122.5 0.7 copy.25
  1123.2 0.4 fusion.25
  1123.6 0.8 fusion.2
  1124.5 249.7 %all-reduce.2 = f32[128,32]{0,1:T(8,128)S(1)} all-reduce(f32[128,32]{0,1:T(8,128)S(1)} %bitcast.158), channel_id=5, replica_groups=mesh['ia'=4,'ja'=16,'ka'=8] {'ia','ja'}, use_global_device_ids=true, to_apply=%region_8.12.clone | all-reduce | flops 4096 | bytes 32768
  1374.2 0.3 fusion.9
  1374.4 0.1 fusion.11
  1374.6 0.2 fusion.37
  1374.8 98.6 %psum.39 = f32[32,32]{1,0:T(8,128)S(1)} all-reduce(f32[32,32]{1,0:T(8,128)S(1)} %fusion.37), channel_id=1, replica_groups=mesh['ia'=4,'ja'=16,'ka'=8] {'ia','ja','ka'}, use_global_device_ids=true, to_apply=%region_9.13 | all-reduce | flops 1024 | bytes 8192 | tf_op jit(solution)/shard_map/psum | solution.py:32
  1473.4 0.7 gather_fusion.2
  1474.1 0.6 multiply_bitcast_fusion
  (14 shorter events, 0.2 us)
Async XLA Ops:
  5.1 0.7 copy-start.2
  5.8 0.7 copy-start.1
  779.1 342.9 %copy-start = (bf16[128,32,128]{2,1,0:T(8,128)(2,1)S(1)}, bf16[128,32,128]{2,1,0:T(8,128)(2,1)}, u32[]{:S(2)}) copy-start(bf16[128,32,128]{2,1,0:T(8,128)(2,1)} %param.8) | copy-start | bytes 3145732
where the time goes:
time: 1480 us; the launch traced here: 1470 us
  blocking collectives  1440 us (97%)
  other arithmetic  22.1 us (1%)
    unnamed x3, blocking collectives  849 us
    psum x3, blocking collectives, owner_update(): gram_raw = lax.psum(gram_of(solved), ('ia', 'ja', 'ka'))  318 us
    psum x1, blocking collectives, local(): lax.psum((gram_of(owned_b), gram_of(owned_c)), ('ia', 'ja', 'ka'))  109 us
    all_gather x1, blocking collectives, collect_a(): return lax.all_gather(owned_a, ('ja', 'ka'), axis=0, tiled=True)  65.1 us
    all_gather x2, blocking collectives, collect_b(): return lax.all_gather(owned_b, ('ia', 'ka'), axis=0, tiled=True)  55.5 us
    all_gather x1, blocking collectives, collect_c(): lax.all_gather(owned_c.astype(jnp.bfloat16), ('ia', 'ja'), axis=0, tiled=...  38.5 us

commit v1 on v0

v1 whole, which is shorter than its diff:
```python
import jax
import jax.numpy as jnp
from jax import lax
from jax.experimental import pallas as pl
from jax.experimental.pallas import tpu as pltpu
from jax.sharding import PartitionSpec as P

HIGH = lax.Precision.HIGHEST
F32 = jnp.float32
BF16 = jnp.bfloat16
R = 32
LANES = 128
PACK = LANES // R


def dot(left, right, dims=((1,), (0,))):
    return lax.dot_general(
        left, right, (dims, ((), ())), precision=HIGH, preferred_element_type=F32
    )


def pack(matrix):
    rows = matrix.shape[0] // PACK
    return jnp.concatenate([matrix[g * rows : (g + 1) * rows] for g in range(PACK)], axis=1)


def unpack(packed):
    return jnp.concatenate([packed[:, g * R : (g + 1) * R] for g in range(PACK)], axis=0)


def eye():
    rows = lax.broadcasted_iota(jnp.int32, (R, R), 0)
    cols = lax.broadcasted_iota(jnp.int32, (R, R), 1)
    return (rows == cols).astype(F32)


def inverse(matrix):
    work = jnp.concatenate([matrix, eye()], axis=1)
    rows = lax.broadcasted_iota(jnp.int32, (R, 1), 0)
    for p in range(R):
        pivot_row = work[p : p + 1, :] / work[p : p + 1, p : p + 1]
        column = work[:, p : p + 1] - (rows == p).astype(F32)
        work = work - column * pivot_row
    return work[:, R : 2 * R]


def scales(gram_raw, total):
    diagonal = gram_raw * eye()
    row = lax.rsqrt(jnp.sum(diagonal, axis=0, keepdims=True) / total + 1e-06)
    column = lax.rsqrt(jnp.sum(diagonal, axis=1, keepdims=True) / total + 1e-06)
    return row, column


def call(kernel, outs, args, flops, scalars=0):
    spec = [pl.BlockSpec(memory_space=pltpu.SMEM)] * scalars
    spec += [pl.BlockSpec(memory_space=pltpu.VMEM)] * (len(args) - scalars)
    moved = sum(4 * a.size for a in args) + sum(4 * o.size for o in outs)
    return pl.pallas_call(
        kernel,
        out_shape=outs,
        in_specs=spec,
        out_specs=[pl.BlockSpec(memory_space=pltpu.VMEM)] * len(outs),
        compiler_params=pltpu.CompilerParams(vmem_limit_bytes=24 * 2**20),
        cost_estimate=pl.CostEstimate(flops=flops, bytes_accessed=moved, transcendentals=0),
    )(*args)


def shape(*dims, dtype=F32):
    return jax.ShapeDtypeStruct(dims, dtype)


def weights_kernel(all_ref, weights_ref, gram_ref):
    rows = all_ref[...]
    products = dot(rows, rows, ((0,), (0,)))
    gram_b = products[0:R, 0:R]
    gram_c = products[R : 2 * R, R : 2 * R] + products[2 * R : 3 * R, 2 * R : 3 * R]
    gram_ref[...] = gram_c
    weights_ref[...] = inverse(gram_b * gram_c)


def first_kernel(sizes, place_ref, all_ref, tensor_ref, send_ref, along_ref):
    n_ia, n_ja, n_ka = sizes
    rows_i, rows_j, rows_k = tensor_ref.shape
    ja, ka = place_ref[1], place_ref[2]
    devices = n_ia * n_ja * n_ka
    k_of = lax.broadcasted_iota(jnp.int32, (rows_k, devices), 0)
    d_of = lax.broadcasted_iota(jnp.int32, (rows_k, devices), 1)
    own = d_of == (k_of >> 1) * n_ka + ka
    odd = (k_of & 1) == 1
    low = all_ref[...].astype(BF16)
    even_rows = jnp.where(own & ~odd, 1.0, 0.0).astype(BF16)
    odd_rows = jnp.where(own & odd, 1.0, 0.0).astype(BF16)
    block_c = jnp.dot(even_rows, low[:, R : 2 * R], preferred_element_type=F32)
    block_c += jnp.dot(odd_rows, low[:, 2 * R : 3 * R], preferred_element_type=F32)
    block_b = jnp.concatenate(
        [
            all_ref[pl.ds(pl.multiple_of((ia * n_ja + ja) * n_ka, n_ka), n_ka), 0:R]
            for ia in range(n_ia)
        ],
        axis=0,
    )
    flat = tensor_ref[...].reshape(rows_i * rows_j, rows_k)
    along = jnp.dot(flat, block_c.astype(BF16), preferred_element_type=F32)
    along_ref[...] = along
    terms = along.reshape(rows_i, rows_j, R) * block_b[None]
    packed = pack(jnp.sum(terms, axis=1))
    half = packed.shape[0] // 2
    peers = send_ref.shape[0] // 2
    send_ref[0:peers] = jnp.broadcast_to(packed[None, :half], (peers, half, LANES))
    send_ref[peers:] = jnp.broadcast_to(packed[None, half:], (peers, half, LANES))


def sum_kernel(got_ref, send_ref):
    total = jnp.sum(got_ref[...], axis=0)
    send_ref[...] = jnp.broadcast_to(total[None], send_ref.shape)


def halves(got):
    pairs = got.shape[0] // 2
    first = got[0]
    second = got[1]
    for n in range(1, pairs):
        first += got[2 * n]
        second += got[2 * n + 1]
    return jnp.concatenate([first, second], axis=0)


def second_kernel(got_ref, weights_ref, along_ref, send_ref, solved_ref):
    summed = unpack(halves(got_ref[...]))
    solved = dot(summed, weights_ref[...])
    solved_ref[...] = solved
    rows_i = solved.shape[0]
    rows_j = along_ref.shape[0] // rows_i
    gram = dot(solved, solved, ((0,), (0,)))
    terms = along_ref[...].reshape(rows_i, rows_j, R) * solved[:, None, :]
    part = jnp.concatenate([pack(jnp.sum(terms, axis=0)), pack(gram)], axis=0)
    send_ref[...] = jnp.broadcast_to(part[None], send_ref.shape)


def third_kernel(
    totals, copies, got_ref, solved_ref, gram_c_ref, turned_ref,
    send_ref, gram_a_ref, gram_b_ref, factor_a_ref, solved_b_ref,
):
    total = jnp.sum(got_ref[...], axis=0)
    half = total.shape[0] // 2
    gram_raw = unpack(total[half:]) * (1.0 / copies)
    row, column = scales(gram_raw, totals[0])
    gram_a = gram_raw * row * column
    gram_a_ref[...] = gram_a
    factor_a = solved_ref[...] * row
    factor_a_ref[...] = factor_a
    summed = unpack(total[:half]) * row
    solved_b = dot(summed, inverse(gram_a * gram_c_ref[...]))
    solved_b_ref[...] = solved_b
    gram_b_ref[...] = pack(dot(solved_b, solved_b, ((0,), (0,))))
    a_low = factor_a.astype(BF16).T
    b_turned = solved_b.T
    part = jnp.zeros((R, turned_ref.shape[2]), F32)
    for j in range(turned_ref.shape[0]):
        along = jnp.dot(a_low, turned_ref[j], preferred_element_type=F32)
        part += along * b_turned[:, j : j + 1]
    half = R // 2
    peers = send_ref.shape[0] // 2
    for n in range(peers):
        send_ref[2 * n] = part[:half]
        send_ref[2 * n + 1] = part[half:]


def pass_kernel(got_ref, gram_ref, send_ref):
    total = jnp.concatenate([jnp.sum(got_ref[...], axis=0), gram_ref[...]], axis=0)
    send_ref[...] = jnp.broadcast_to(total[None], send_ref.shape)


def fourth_kernel(
    totals, sizes, place_ref, got_ref, gram_a_ref, factor_a_ref, solved_b_ref,
    send_ref, out_a_ref, out_b_ref, own_c_ref,
):
    n_ia, n_ja, n_ka = sizes
    ia, ja, ka = place_ref[0], place_ref[1], place_ref[2]
    half = R // 2
    summed = halves(got_ref[:, 0:half, :])
    gram_raw = unpack(jnp.sum(got_ref[:, half:, :], axis=0))
    row, column = scales(gram_raw, totals[1])
    gram_b = gram_raw * row * column
    out_a_ref[...] = factor_a_ref[pl.ds(ja * n_ka + ka, 1), :]
    out_b_ref[...] = solved_b_ref[pl.ds(ia * n_ka + ka, 1), :] * row
    solved = dot(inverse(gram_a_ref[...] * gram_b), summed * column)
    squares = dot(jnp.ones((8, solved.shape[1]), F32), solved * solved, ((1,), (1,)))
    squares = jnp.concatenate([squares, jnp.zeros((8, LANES - R), F32)], axis=1)
    send_ref[...] = jnp.broadcast_to(squares[None], send_ref.shape)
    k_of = lax.broadcasted_iota(jnp.int32, (8, solved.shape[1]), 1)
    t_of = lax.broadcasted_iota(jnp.int32, (8, solved.shape[1]), 0)
    chosen = jnp.where(k_of == 2 * (ia * n_ja + ja) + t_of, 1.0, 0.0)
    own_c_ref[...] = dot(chosen, solved, ((1,), (1,)))


def last_kernel(total, got_ref, own_c_ref, out_ref):
    squares = jnp.sum(got_ref[...], axis=0)[0:1, 0:R]
    out_ref[...] = own_c_ref[0:2, :] * lax.rsqrt(squares / total + 1e-06)


def exchange(blocks, axes, groups=None):
    return lax.all_to_all(blocks, axes, 0, 0, tiled=True, axis_index_groups=groups)


def local(tensor, factor_b, factor_c):
    rows_i, rows_j, rows_k = tensor.shape
    sizes = tuple(lax.axis_size(axis) for axis in ("ia", "ja", "ka"))
    n_ia, n_ja, n_ka = sizes
    totals = (rows_i * n_ia, rows_j * n_ja, rows_k * n_ka)
    devices = n_ia * n_ja * n_ka
    cores = 2
    place = jnp.stack([lax.axis_index(axis) for axis in ("ia", "ja", "ka")]).astype(jnp.int32)
    plane = [
        [(z * cores + core) * n_ka + y for core in range(cores) for y in range(n_ka)]
        for z in range(n_ja // cores)
    ]
    line = [
        [x * n_ja + z * cores + core for x in range(n_ia) for core in range(cores)]
        for z in range(n_ja // cores)
    ]
    own = jnp.concatenate(
        [factor_b.reshape(1, R), factor_c.reshape(1, 2 * R), jnp.zeros((1, R), F32)], axis=1
    )
    rows = exchange(jnp.broadcast_to(own, (devices, LANES)), ("ia", "ja", "ka"))
    turned = jnp.transpose(tensor, (1, 0, 2))
    weights_a, gram_c = call(
        weights_kernel, [shape(R, R), shape(R, R)], [rows], 2**24
    )
    send, along = call(
        lambda *refs: first_kernel(sizes, *refs),
        [shape(cores * n_ka, R // 2, LANES), shape(rows_i * rows_j, R)],
        [place, rows, tensor],
        2**26,
        scalars=1,
    )
    got = exchange(send, ("ja", "ka"), plane)
    (send,) = call(sum_kernel, [shape(n_ja, R // 2, LANES)], [got], 2**16)
    got = exchange(send, "ja")
    send, solved_a = call(
        second_kernel, [shape(n_ia * n_ka, 16, LANES), shape(rows_i, R)], [got, weights_a, along], 2**24
    )
    got = exchange(send, ("ia", "ka"))
    send, gram_a, gram_b, factor_a, solved_b = call(
        lambda *refs: third_kernel(totals, n_ka, *refs),
        [
            shape(n_ia * cores, R // 2, LANES),
            shape(R, R),
            shape(R // PACK, LANES),
            shape(rows_i, R),
            shape(rows_j, R),
        ],
        [got, solved_a, gram_c, turned],
        2**26,
    )
    got = exchange(send, ("ia", "ja"), line)
    (send,) = call(pass_kernel, [shape(n_ja, 24, LANES)], [got, gram_b], 2**16)
    got = exchange(send, "ja")
    send, out_a, out_b, own_c = call(
        lambda *refs: fourth_kernel(totals, sizes, *refs),
        [shape(n_ka, 8, LANES), shape(1, R), shape(1, R), shape(8, R)],
        [place, got, gram_a, factor_a, solved_b],
        2**22,
        scalars=1,
    )
    got = exchange(send, "ka")
    (out_c,) = call(
        lambda *refs: last_kernel(totals[2], *refs), [shape(2, R)], [got, own_c], 2**12
    )
    return out_a[None], out_b[None], out_c[None]


def solution(mesh):
    placed = (P("ia", "ja", "ka"), P("ja", ("ia", "ka"), None), P("ka", ("ia", "ja"), None))
    return jax.shard_map(
        local,
        mesh=mesh,
        in_specs=placed,
        out_specs=(
            P("ia", ("ja", "ka"), None),
            P("ja", ("ia", "ka"), None),
            P("ka", ("ia", "ja"), None),
        ),
        check_vma=False,
    )
```

time: 1480 us -> 130 us (0.09)
  blocking collectives: 1440 us -> 43.6 us
  waiting for transfers between devices: 0 us -> 32.5 us
  starting transfers between devices: 0 us -> 31.2 us
  other arithmetic: 22.1 us -> 0.81 us
    unnamed x3 -> x0, blocking collectives: 849 us -> none
    psum x4 -> x0, blocking collectives: 427 us -> none  [the longest x3 318 us: owner_update(): gram_raw = lax.psum(gram_of(solved), ('ia', 'ja', 'ka'))]
    all_gather x4 -> x0, blocking collectives: 159 us -> none  [the longest x1 65.1 us: collect_a(): return lax.all_gather(owned_a, ('ja', 'ka'), axis=0, tiled=True)]
    all_to_all x0 -> x4, blocking collectives: none -> 43.6 us  [exchange(): lax.all_to_all(blocks, axes, 0, 0, tiled=True, axis_index_groups=groups)]
    all_to_all x0 -> x3, waiting for transfers between devices: none -> 32.5 us  [exchange(): lax.all_to_all(blocks, axes, 0, 0, tiled=True, axis_index_groups=groups)]
    all_to_all x0 -> x3, starting transfers between devices: none -> 31.2 us  [exchange(): lax.all_to_all(blocks, axes, 0, 0, tiled=True, axis_index_groups=groups)]
    another operation x15 -> x1, other arithmetic: 20.1 us -> 0.08 us  [local(): jnp.stack([lax.axis_index(axis) for axis in ('ia', 'ja', 'ka')])]
  transfers between devices with their start and end apart: 0 -> 3, of which waited for: 0 -> 3; matrix products, arithmetic and copies ran while one was open for 0% -> 0% of each run, Pallas kernels for 0% -> 3%
where the time goes in v1:
time: 130 us; the launch traced here: 129 us
  blocking collectives  43.6 us (34%)
  waiting for transfers between devices  32.5 us (25%)
  starting transfers between devices  31.2 us (24%)
  Pallas kernels  13.6 us (10%)
  local copies, waits for them, and re-layouts  6.57 us (5%)
    all_to_all x4, blocking collectives, exchange(): lax.all_to_all(blocks, axes, 0, 0, tiled=True, axis_index_groups=groups)  43.6 us
    all_to_all x3, waiting for transfers between devices, exchange(): lax.all_to_all(blocks, axes, 0, 0, tiled=True, axis_index_groups=groups)  32.5 us
    all_to_all x3, starting transfers between devices, exchange(): lax.all_to_all(blocks, axes, 0, 0, tiled=True, axis_index_groups=groups)  31.2 us
    pallas_call x8, Pallas kernels, call(): pl.pallas_call(kernel, out_shape=outs, in_specs=spec, out_specs=[pl.Block...  13.6 us
    unnamed x21, local copies, waits for them, and re-layouts  4.97 us
  transfers between devices with their start and end apart: 3, of which 3 were waited for; matrix products, arithmetic and copies ran while one was open for 0% of the time, Pallas kernels for 3%

profile of v1, /device:TPU:1, one launch (start us, length us, event | category | flops | bytes accessed | tf_op | source)
XLA Modules:
  0.0 129.0 jit_solution(9153297010351041472)
XLA Ops:
  0.6 0.8 reshape.19
  1.4 0.7 fusion
  2.1 0.8 broadcast_in_dim.18
  3.0 22.2 %all-to-all-start = ((f32[512,1,128]{2,1,0:T(1,128)}), f32[512,1,128]{2,1,0:T(1,128)S(1)}, u32[]{:S(2)}, u32[]{:S(2)}) async-start(f32[512,1,128]{2,1,0:T(1,128)} %broadcast_in_dim.18), calls=%async_computation | async-start | bytes 524288 | tf_op jit(solution)/shard_map/all_to_all | solution.py:203
  25.1 0.1 pad_add_fusion.refs_0_
  25.2 0.0 copy-start.8
  25.2 16.9 %all-to-all-done = f32[512,1,128]{2,1,0:T(1,128)S(1)} async-done(((f32[512,1,128]{2,1,0:T(1,128)}), f32[512,1,128]{2,1,0:T(1,128)S(1)}, u32[]{:S(2)}, u32[]{:S(2)}) %all-to-all-start) | async-done | bytes 262176 | tf_op jit(solution)/shard_map/all_to_all | solution.py:203
  42.1 0.0 copy-start
  42.1 1.2 copy-done
  43.4 1.4 %shard_map.58 = (f32[16,16,128]{2,1,0:T(8,128)S(1)}, f32[4096,32]{1,0:T(8,128)S(1)}) custom-call(s32[3]{0:T(128)S(1)} %pad_add_fusion.refs_0_, f32[512,128]{1,0:T(8,128)S(1)} %bitcast.18, bf16[128,32,128]{2,1,0:T(8,128)(2,1)S(1)} %copy-done), custom_call_target="tpu_custom_call" | custom-call | flops 67108864 | bytes 3014668 | tf_op jit(solution)/shard_map/pallas_call | solution.py:58
  44.7 0.0 copy-start.1
  44.7 10.5 %all_to_all.38.got_ref = f32[16,16,128]{2,1,0:T(8,128)S(1)} all-to-all(f32[16,16,128]{2,1,0:T(8,128)S(1)} %get-tuple-element.18), channel_id=1, replica_groups={{0,1,2,3,4,5,6,7,8,9,10,11,12,13,14,15},{16,17,18,19,20,21,22,23,24,25,..., dimensions={0} | all-to-all | bytes 262144 | tf_op jit(solution)/shard_map/all_to_all | solution.py:203
  55.2 0.0 copy-start.2
  55.3 0.6 copy-done.2
  55.9 0.0 copy-done.8
  55.9 4.7 %all-to-all-start.2 = ((f32[16,16,128]{2,1,0:T(8,128)}), f32[16,16,128]{2,1,0:T(8,128)S(1)}, u32[]{:S(2)}, u32[]{:S(2)}) async-start(f32[16,16,128]{2,1,0:T(8,128)} %copy-done.2), calls=%async_computation.2 | async-start | bytes 262144 | tf_op jit(solution)/shard_map/all_to_all | solution.py:203
  60.6 3.3 %shard_map.60 = (f32[32,32]{1,0:T(8,128)S(1)}, f32[32,32]{1,0:T(8,128)S(1)}) custom-call(f32[512,128]{1,0:T(8,128)S(1)} %bitcast.19), custom_call_target="tpu_custom_call" | custom-call | flops 16777216 | bytes 270336 | tf_op jit(solution)/shard_map/pallas_call | solution.py:58
  63.8 0.0 copy-start.6
  63.8 0.6 copy-done.6
  64.5 5.3 %all-to-all-done.2.got_ref = f32[16,16,128]{2,1,0:T(8,128)S(1)} async-done(((f32[16,16,128]{2,1,0:T(8,128)}), f32[16,16,128]{2,1,0:T(8,128)S(1)}, u32[]{:S(2)}, u32[]{:S(2)}) %all-to-all-start.2) | async-done | bytes 131104 | tf_op jit(solution)/shard_map/all_to_all | solution.py:203
  69.7 0.0 copy-start.7
  69.7 0.7 copy-done.7
  70.4 0.8 shard_map.61
  71.2 0.0 copy-start.3
  71.3 0.7 copy-done.3
  71.9 0.0 copy-start.4
  72.0 0.6 copy-done.4
  72.6 0.0 copy-start.5
  72.6 4.4 %all-to-all-start.3 = ((f32[32,16,128]{2,1,0:T(8,128)}), f32[32,16,128]{2,1,0:T(8,128)S(1)}, u32[]{:S(2)}, u32[]{:S(2)}) async-start(f32[32,16,128]{2,1,0:T(8,128)} %copy-done.3), calls=%async_computation.3 | async-start | bytes 524288 | tf_op jit(solution)/shard_map/all_to_all | solution.py:203
  77.0 0.0 copy-done.1
  77.0 0.0 copy-start.9
  77.0 0.4 copy.9
  77.4 10.3 %all-to-all-done.3.refs_0_ = f32[32,16,128]{2,1,0:T(8,128)S(1)} async-done(((f32[32,16,128]{2,1,0:T(8,128)}), f32[32,16,128]{2,1,0:T(8,128)S(1)}, u32[]{:S(2)}, u32[]{:S(2)}) %all-to-all-start.3) | async-done | bytes 262176 | tf_op jit(solution)/shard_map/all_to_all | solution.py:203
  87.7 0.0 copy-done.5
  87.7 3.5 %shard_map.62 = (f32[8,16,128]{2,1,0:T(8,128)S(1)}, f32[32,32]{1,0:T(8,128)S(1)}, f32[8,128]{1,0:T(8,128)S(1)}, f32[128,32]{1,0:T(8,128)S(1)}, f32[32,32]{1,0:T(8,128)S(1)}) custom-call(f32[32,16,128]{2,1,0:T(8,128)S(1)} %all-to-all-done.3.refs_0_, f32[128,32]{1,0:T(8,128)S(1)} %copy-done.5, f32[32,32]{1,0:T(8,128)S(1)} %get-tuple-element.23.refs_2_, ...), custom_call_target="tpu_custom_call" | custom-call | flops 67108864 | bytes 2473984 | tf_op jit(solution)/shard_map/pallas_call | solution.py:58
  91.2 9.9 %all_to_all.39.got_ref = f32[8,16,128]{2,1,0:T(8,128)S(1)} all-to-all(f32[8,16,128]{2,1,0:T(8,128)S(1)} %get-tuple-element.24), channel_id=1, replica_groups={{0,8,128,136,256,264,384,392},{16,24,144,152,272,280,400,408},{32,40,16..., dimensions={0} | all-to-all | bytes 131072 | tf_op jit(solution)/shard_map/all_to_all | solution.py:203
  101.2 13.6 %all_to_all.40.refs_1_ = f32[16,24,128]{2,1,0:T(8,128)S(1)} all-to-all(f32[16,24,128]{2,1,0:T(8,128)S(1)} %shard_map.63), channel_id=1, replica_groups=mesh['ia'=4,'ja'=16,'ka'=8] {'ja'}, dimensions={0} | all-to-all | bytes 393216 | tf_op jit(solution)/shard_map/all_to_all | solution.py:203
  114.8 0.0 copy-done.9
  114.8 4.1 %shard_map.64 = (f32[8,8,128]{2,1,0:T(8,128)S(1)}, f32[1,32]{1,0:T(1,128)}, f32[1,32]{1,0:T(1,128)}, f32[8,32]{1,0:T(8,128)S(1)}) custom-call(s32[3]{0:T(128)S(1)} %copy-done.9, f32[16,24,128]{2,1,0:T(8,128)S(1)} %all_to_all.40.refs_1_, f32[32,32]{1,0:T(8,128)S(1)} %get-tuple-element.26.refs_2_, f32[128,32]{1,0:T(8,128)S(1)} %get-tuple-element.27.refs_3_, ...), custom_call_target="tpu_custom_call" | custom-call | flops 4194304 | bytes 255244 | tf_op jit(solution)/shard_map/pallas_call | solution.py:58
  118.8 9.6 %all_to_all.41.refs_0_ = f32[8,8,128]{2,1,0:T(8,128)S(1)} all-to-all(f32[8,8,128]{2,1,0:T(8,128)S(1)} %get-tuple-element.31), channel_id=1, replica_groups=mesh['ia'=4,'ja'=16,'ka'=8] {'ka'}, dimensions={0} | all-to-all | bytes 65536 | tf_op jit(solution)/shard_map/all_to_all | solution.py:203
  128.5 0.6 shard_map.65
  (3 shorter events, 0.0 us)
Async XLA Ops:
  3.0 39.2 %all-to-all-start = ((f32[512,1,128]{2,1,0:T(1,128)}), f32[512,1,128]{2,1,0:T(1,128)S(1)}, u32[]{:S(2)}, u32[]{:S(2)}) async-start(f32[512,1,128]{2,1,0:T(1,128)} %broadcast_in_dim.18), calls=%async_computation | async-start | bytes 524288 | tf_op jit(solution)/shard_map/all_to_all | solution.py:203
  25.2 30.7 %copy-start.8 = (s32[3]{0:T(128)}, s32[3]{0:T(128)S(1)}, u32[]{:S(2)}) copy-start(s32[3]{0:T(128)S(1)} %pad_add_fusion.refs_0_) | copy-start | bytes 40
  42.1 1.2 copy-start
  44.7 32.3 %copy-start.1 = (bf16[128,32,128]{2,1,0:T(8,128)(2,1)S(1)}, bf16[128,32,128]{2,1,0:T(8,128)(2,1)}, u32[]{:S(2)}) copy-start(bf16[128,32,128]{2,1,0:T(8,128)(2,1)} %refs_2_.1) | copy-start | bytes 3145732
  55.2 0.6 copy-start.2
  55.9 13.8 %all-to-all-start.2 = ((f32[16,16,128]{2,1,0:T(8,128)}), f32[16,16,128]{2,1,0:T(8,128)S(1)}, u32[]{:S(2)}, u32[]{:S(2)}) async-start(f32[16,16,128]{2,1,0:T(8,128)} %copy-done.2), calls=%async_computation.2 | async-start | bytes 262144 | tf_op jit(solution)/shard_map/all_to_all | solution.py:203
  63.8 0.6 copy-start.6
  69.7 0.7 copy-start.7
  71.2 0.7 copy-start.3
  71.9 0.6 copy-start.4
  72.6 15.1 %copy-start.5 = (f32[128,32]{1,0:T(8,128)S(1)}, f32[128,32]{1,0:T(8,128)}, u32[]{:S(2)}) copy-start(f32[128,32]{1,0:T(8,128)} %copy-done.4) | copy-start | bytes 49156
  72.6 15.1 %all-to-all-start.3 = ((f32[32,16,128]{2,1,0:T(8,128)}), f32[32,16,128]{2,1,0:T(8,128)S(1)}, u32[]{:S(2)}, u32[]{:S(2)}) async-start(f32[32,16,128]{2,1,0:T(8,128)} %copy-done.3), calls=%async_computation.3 | async-start | bytes 524288 | tf_op jit(solution)/shard_map/all_to_all | solution.py:203
  77.0 37.8 %copy-start.9 = (s32[3]{0:T(128)S(1)}, s32[3]{0:T(128)}, u32[]{:S(2)}) copy-start(s32[3]{0:T(128)} %copy-done.8) | copy-start | bytes 40

commit v2 on v1

v2 whole, which is shorter than its diff:
```python
import jax
import jax.numpy as jnp
from jax import lax
from jax.experimental import pallas as pl
from jax.experimental.pallas import tpu as pltpu
from jax.sharding import PartitionSpec as P

HIGH = lax.Precision.HIGHEST
F32 = jnp.float32
BF16 = jnp.bfloat16
R = 32
LANES = 128
PACK = LANES // R
SUB = R // PACK


def dot(left, right, dims=((1,), (0,))):
    return lax.dot_general(
        left, right, (dims, ((), ())), precision=HIGH, preferred_element_type=F32
    )


def pack(matrix):
    rows = matrix.shape[0] // PACK
    return jnp.concatenate([matrix[g * rows : (g + 1) * rows] for g in range(PACK)], axis=1)


def unpack(packed):
    return jnp.concatenate([packed[:, g * R : (g + 1) * R] for g in range(PACK)], axis=0)


def lane_groups(matrix):
    total = matrix[0:R, 0:R]
    for g in range(1, PACK):
        total += matrix[g * R : (g + 1) * R, g * R : (g + 1) * R]
    return total


def eye():
    rows = lax.broadcasted_iota(jnp.int32, (R, R), 0)
    cols = lax.broadcasted_iota(jnp.int32, (R, R), 1)
    return (rows == cols).astype(F32)


def inverse(packed):
    work = packed
    lane = lax.broadcasted_iota(jnp.int32, (SUB, LANES), 1)
    sub = lax.broadcasted_iota(jnp.int32, (SUB, LANES), 0)
    group, place = lane // R, lane % R
    for p in range(PACK):
        in_rows = group == p
        in_cols = place // SUB == p
        spread = [jnp.broadcast_to(work[s : s + 1, :], (SUB, LANES)) for s in range(SUB)]
        cols = [
            jnp.where(
                in_rows,
                jnp.where(sub == s, -1.0, 0.0),
                jnp.take_along_axis(work, group * R + p * SUB + s, axis=1),
            )
            for s in range(SUB)
        ]
        rows = [
            jnp.where(
                in_cols,
                jnp.where(place == p * SUB + s, 1.0, 0.0),
                jnp.take_along_axis(spread[s], p * R + place, axis=1),
            )
            for s in range(SUB)
        ]
        pivots = [[None] * SUB for _ in range(SUB)]
        for s in range(SUB):
            for t in range(s, SUB):
                where = jnp.full((SUB, LANES), p * R + p * SUB + t, jnp.int32)
                pivots[s][t] = pivots[t][s] = jnp.take_along_axis(spread[s], where, axis=1)
        for t in range(SUB):
            recip = 1.0 / pivots[t][t]
            rows[t] = rows[t] * recip
            for u in range(t + 1, SUB):
                pivots[t][u] = pivots[t][u] * recip
            for s in range(SUB):
                if s != t:
                    factor = pivots[s][t]
                    rows[s] = rows[s] - factor * rows[t]
                    for u in range(t + 1, SUB):
                        pivots[s][u] = pivots[s][u] - factor * pivots[t][u]
        work = jnp.where(in_rows | in_cols, 0.0, work)
        for col, row in zip(cols, rows):
            work = work - col * row
    return work


def scales(gram_raw, total):
    diagonal = gram_raw * eye()
    row = lax.rsqrt(jnp.sum(diagonal, axis=0, keepdims=True) / total + 1e-06)
    column = lax.rsqrt(jnp.sum(diagonal, axis=1, keepdims=True) / total + 1e-06)
    return row, column


def call(kernel, outs, args, flops, scalars=0):
    spec = [pl.BlockSpec(memory_space=pltpu.SMEM)] * scalars
    spec += [pl.BlockSpec(memory_space=pltpu.VMEM)] * (len(args) - scalars)
    moved = sum(4 * a.size for a in args) + sum(4 * o.size for o in outs)
    return pl.pallas_call(
        kernel,
        out_shape=outs,
        in_specs=spec,
        out_specs=[pl.BlockSpec(memory_space=pltpu.VMEM)] * len(outs),
        compiler_params=pltpu.CompilerParams(vmem_limit_bytes=24 * 2**20),
        cost_estimate=pl.CostEstimate(flops=flops, bytes_accessed=moved, transcendentals=0),
    )(*args)


def shape(*dims, dtype=F32):
    return jax.ShapeDtypeStruct(dims, dtype)


def own_kernel(b_ref, c_ref, send_ref):
    row = jnp.concatenate(
        [b_ref[...], c_ref[0:1, :], c_ref[1:2, :], jnp.zeros((1, LANES - 3 * R), F32)], axis=1
    )
    send_ref[...] = jnp.broadcast_to(row, send_ref.shape)


def along_kernel(sizes, place_ref, rows_ref, tensor_ref, send_ref):
    n_ia, n_ja, n_ka = sizes
    rows_i, rows_j, rows_k = tensor_ref.shape
    ja = place_ref[1]
    rows = rows_ref[...]
    sources = rows.shape[0]
    k_of = lax.broadcasted_iota(jnp.int32, (rows_k, sources), 0)
    d_of = lax.broadcasted_iota(jnp.int32, (rows_k, sources), 1)
    low = rows.astype(BF16)
    even = jnp.where(k_of == 2 * d_of, 1.0, 0.0).astype(BF16)
    odd = jnp.where(k_of == 2 * d_of + 1, 1.0, 0.0).astype(BF16)
    block_c = jnp.dot(even, low[:, R : 2 * R], preferred_element_type=F32)
    block_c += jnp.dot(odd, low[:, 2 * R : 3 * R], preferred_element_type=F32)
    tiled = jnp.concatenate([block_c] * PACK, axis=1)
    lane = lax.broadcasted_iota(jnp.int32, (rows_k, LANES), 1) // R
    weights = jnp.concatenate(
        [jnp.where(lane == g, tiled, 0.0).astype(BF16) for g in range(PACK)], axis=0
    )
    low_i = rows_i // (PACK * n_ka)
    sums = low_i * rows_j
    for ka in range(n_ka):
        left = jnp.concatenate(
            [
                tensor_ref[(g * n_ka + ka) * low_i : (g * n_ka + ka + 1) * low_i].reshape(sums, rows_k)
                for g in range(PACK)
            ],
            axis=1,
        )
        send_ref[ka, 0:sums, :] = jnp.dot(left, weights, preferred_element_type=F32)
    products = dot(rows, rows, ((0,), (0,)))
    gram_b = products[0:R, 0:R]
    gram_c = products[R : 2 * R, R : 2 * R] + products[2 * R : 3 * R, 2 * R : 3 * R]
    own_b = jnp.concatenate(
        [rows_ref[pl.ds(ia * n_ja + ja, 1), 0:R] for ia in range(n_ia)], axis=1
    )
    upper = lax.broadcasted_iota(jnp.int32, (R, R), 0) <= lax.broadcasted_iota(jnp.int32, (R, R), 1)
    diagonal = jnp.sum(gram_c * eye(), axis=0, keepdims=True)
    riders = jnp.concatenate(
        [
            pack(jnp.where(upper, gram_b, gram_c)),
            own_b,
            jnp.concatenate([diagonal, jnp.zeros((1, LANES - R), F32)], axis=1),
            jnp.zeros((SUB - 2, LANES), F32),
        ],
        axis=0,
    )
    for ka in range(n_ka):
        send_ref[ka, sums:, :] = riders


def first_kernel(low_i, got_ref, send_ref, along_ref, grams_ref):
    sums = got_ref.shape[1] - 2 * SUB
    along = jnp.sum(got_ref[:, 0:sums, :], axis=0)
    along_ref[...] = along
    grams_ref[...] = jnp.sum(got_ref[:, sums:, :], axis=0)
    own_b = jnp.concatenate(
        [got_ref[ka, sums + SUB : sums + SUB + 1, :] for ka in range(got_ref.shape[0])], axis=0
    )
    block_b = unpack(own_b)
    rows_j = block_b.shape[0]
    wide_b = jnp.concatenate([block_b] * PACK, axis=1)
    terms = along.reshape(low_i, rows_j, LANES) * wide_b[None]
    summed = jnp.concatenate(
        [jnp.sum(terms, axis=1), jnp.zeros((8 - low_i, LANES), F32)], axis=0
    )
    send_ref[...] = jnp.broadcast_to(summed[None], send_ref.shape)


def weights_kernel(grams_ref, weights_ref, gram_ref):
    mixed = unpack(grams_ref[0:SUB])
    turned = mixed.T
    rows = lax.broadcasted_iota(jnp.int32, (R, R), 0)
    cols = lax.broadcasted_iota(jnp.int32, (R, R), 1)
    gram_b = jnp.where(rows <= cols, mixed, turned)
    gram_c = jnp.where(rows > cols, mixed, jnp.where(rows == cols, grams_ref[SUB + 1 : SUB + 2, 0:R], turned))
    gram_ref[...] = gram_c
    one = unpack(inverse(pack(gram_b * gram_c)))
    tiled = jnp.concatenate([jnp.concatenate([one] * PACK, axis=1)] * PACK, axis=0)
    rows = lax.broadcasted_iota(jnp.int32, (LANES, LANES), 0) // R
    cols = lax.broadcasted_iota(jnp.int32, (LANES, LANES), 1) // R
    weights_ref[...] = jnp.where(rows == cols, tiled, 0.0)


def second_kernel(low_i, got_ref, weights_ref, along_ref, send_ref):
    summed = jnp.sum(got_ref[...], axis=0)
    solved = dot(summed, weights_ref[...])[0:low_i]
    rows_j = along_ref.shape[0] // low_i
    terms = along_ref[...].reshape(low_i, rows_j, LANES) * solved[:, None, :]
    wide = jnp.sum(terms, axis=0)
    part = wide[:, 0:R]
    for g in range(1, PACK):
        part += wide[:, g * R : (g + 1) * R]
    rows = jnp.concatenate([pack(part), solved], axis=0)
    send_ref[...] = jnp.broadcast_to(rows[None], send_ref.shape)


def third_kernel(
    totals, sizes, place_ref, got_ref, gram_c_ref, turned_ref,
    send_ref, gram_a_ref, factor_a_ref, solved_b_ref,
):
    n_ia, n_ja, n_ka = sizes
    ia = place_ref[0]
    peers, _, _ = got_ref.shape
    low_i = got_ref.shape[1] - SUB
    total = jnp.sum(got_ref[:, 0:SUB, :], axis=0)
    everyone = jnp.concatenate([got_ref[n, SUB:, :] for n in range(peers)], axis=0)
    gram_raw = lane_groups(dot(everyone, everyone, ((0,), (0,))))
    row, column = scales(gram_raw, totals[0])
    gram_a = gram_raw * row * column
    gram_a_ref[...] = gram_a
    solved_a = unpack(
        jnp.concatenate([got_ref[ia * n_ka + ka, SUB:, :] for ka in range(n_ka)], axis=0)
    )
    factor_a = solved_a * row
    factor_a_ref[...] = factor_a
    summed = unpack(total) * row
    solved_b = dot(summed, unpack(inverse(pack(gram_a * gram_c_ref[...]))))
    solved_b_ref[...] = solved_b
    gram_b = pack(dot(solved_b, solved_b, ((0,), (0,))))
    a_low = factor_a.astype(BF16).T
    b_turned = solved_b.T
    part = jnp.zeros((R, turned_ref.shape[2]), F32)
    for j in range(turned_ref.shape[0]):
        along = jnp.dot(a_low, turned_ref[j], preferred_element_type=F32)
        part += along * b_turned[:, j : j + 1]
    half = R // 2
    first = jnp.concatenate([part[:half], gram_b], axis=0)
    second = jnp.concatenate([part[half:], gram_b], axis=0)
    for n in range(n_ja // 2):
        send_ref[2 * n] = first
        send_ref[2 * n + 1] = second


def pass_kernel(got_ref, send_ref, gram_ref):
    total = jnp.sum(got_ref[...], axis=0)
    half = R // 2
    gram_ref[...] = total[half:]
    send_ref[...] = jnp.broadcast_to(total[None, :half], send_ref.shape)


def last_weights_kernel(totals, sizes, place_ref, gram_b_ref, gram_a_ref, factor_a_ref, solved_b_ref,
                        weights_ref, out_a_ref, out_b_ref):
    n_ia, n_ja, n_ka = sizes
    ia, ja, ka = place_ref[0], place_ref[1], place_ref[2]
    gram_raw = unpack(gram_b_ref[...])
    row, column = scales(gram_raw, totals[1])
    gram_b = gram_raw * row * column
    out_a_ref[...] = factor_a_ref[pl.ds(ja * n_ka + ka, 1), :]
    out_b_ref[...] = solved_b_ref[pl.ds(ia * n_ka + ka, 1), :] * row
    weights_ref[...] = unpack(inverse(pack(gram_a_ref[...] * gram_b))) * row


def fourth_kernel(sizes, place_ref, got_ref, weights_ref, send_ref, own_c_ref):
    n_ia, n_ja, n_ka = sizes
    ia, ja = place_ref[0], place_ref[1]
    first = got_ref[0]
    second = got_ref[1]
    for n in range(1, n_ia):
        first += got_ref[2 * n]
        second += got_ref[2 * n + 1]
    solved = dot(weights_ref[...], jnp.concatenate([first, second], axis=0))
    squares = dot(jnp.ones((8, solved.shape[1]), F32), solved * solved, ((1,), (1,)))
    squares = jnp.concatenate([squares, jnp.zeros((8, LANES - R), F32)], axis=1)
    send_ref[...] = jnp.broadcast_to(squares[None], send_ref.shape)
    k_of = lax.broadcasted_iota(jnp.int32, (8, solved.shape[1]), 1)
    t_of = lax.broadcasted_iota(jnp.int32, (8, solved.shape[1]), 0)
    chosen = jnp.where(k_of == 2 * (ia * n_ja + ja) + t_of, 1.0, 0.0)
    own_c_ref[...] = dot(chosen, solved, ((1,), (1,)))


def last_kernel(total, got_ref, own_c_ref, out_ref):
    squares = jnp.sum(got_ref[...], axis=0)[0:1, 0:R]
    out_ref[...] = own_c_ref[0:2, :] * lax.rsqrt(squares / total + 1e-06)


def exchange(blocks, axes, groups=None):
    return lax.all_to_all(blocks, axes, 0, 0, tiled=True, axis_index_groups=groups)


def local(tensor, factor_b, factor_c):
    rows_i, rows_j, rows_k = tensor.shape
    sizes = tuple(lax.axis_size(axis) for axis in ("ia", "ja", "ka"))
    n_ia, n_ja, n_ka = sizes
    totals = (rows_i * n_ia, rows_j * n_ja, rows_k * n_ka)
    cores = 2
    low_i = rows_i // (PACK * n_ka)
    place = jnp.stack([lax.axis_index(axis) for axis in ("ia", "ja", "ka")]).astype(jnp.int32)
    line = [
        [x * n_ja + z * cores + core for x in range(n_ia) for core in range(cores)]
        for z in range(n_ja // cores)
    ]
    (send,) = call(own_kernel, [shape(n_ia * n_ja, LANES)], [factor_b[0], factor_c[0]], 2**10)
    rows = exchange(send, ("ia", "ja"))
    turned = jnp.transpose(tensor, (1, 0, 2))
    rows, turned = lax.optimization_barrier((rows, turned))
    (send,) = call(
        lambda *refs: along_kernel(sizes, *refs),
        [shape(n_ka, low_i * rows_j + 2 * SUB, LANES)],
        [place, rows, tensor],
        2**26,
        scalars=1,
    )
    got = exchange(send, "ka")
    send, along, grams = call(
        lambda *refs: first_kernel(low_i, *refs),
        [shape(n_ja, 8, LANES), shape(low_i * rows_j, LANES), shape(2 * SUB, LANES)],
        [got],
        2**20,
    )
    got = exchange(send, "ja")
    weights_a, gram_c = call(weights_kernel, [shape(LANES, LANES), shape(R, R)], [grams], 2**24)
    (send,) = call(
        lambda *refs: second_kernel(low_i, *refs),
        [shape(n_ia * n_ka, SUB + low_i, LANES)],
        [got, weights_a, along],
        2**20,
    )
    got = exchange(send, ("ia", "ka"))
    send, gram_a, factor_a, solved_b = call(
        lambda *refs: third_kernel(totals, sizes, *refs),
        [
            shape(n_ja, R // 2 + SUB, LANES),
            shape(R, R),
            shape(rows_i, R),
            shape(rows_j, R),
        ],
        [place, got, gram_c, turned],
        2**26,
        scalars=1,
    )
    got = exchange(send, "ja")
    send, gram_b = call(
        pass_kernel, [shape(n_ia * cores, R // 2, LANES), shape(SUB, LANES)], [got], 2**16
    )
    got = exchange(send, ("ia", "ja"), line)
    weights_c, out_a, out_b = call(
        lambda *refs: last_weights_kernel(totals, sizes, *refs),
        [shape(R, R), shape(1, R), shape(1, R)],
        [place, gram_b, gram_a, factor_a, solved_b],
        2**24,
        scalars=1,
    )
    send, own_c = call(
        lambda *refs: fourth_kernel(sizes, *refs),
        [shape(n_ka, 8, LANES), shape(8, R)],
        [place, got, weights_c],
        2**20,
        scalars=1,
    )
    got = exchange(send, "ka")
    (out_c,) = call(
        lambda *refs: last_kernel(totals[2], *refs), [shape(2, R)], [got, own_c], 2**12
    )
    return out_a[None], out_b[None], out_c[None]


def solution(mesh):
    placed = (P("ia", "ja", "ka"), P("ja", ("ia", "ka"), None), P("ka", ("ia", "ja"), None))
    return jax.shard_map(
        local,
        mesh=mesh,
        in_specs=placed,
        out_specs=(
            P("ia", ("ja", "ka"), None),
            P("ja", ("ia", "ka"), None),
            P("ka", ("ia", "ja"), None),
        ),
        check_vma=False,
    )
```

time: 130 us -> 118 us (0.908)
  blocking collectives: 43.6 us -> 62.1 us
  waiting for transfers between devices: 32.5 us -> 17.2 us
  starting transfers between devices: 31.2 us -> 24.2 us
  local copies, waits for them, and re-layouts: 6.57 us -> 2.39 us
  Pallas kernels: 13.6 us -> 10.8 us
    all_to_all x4, blocking collectives: 43.6 us -> 62.1 us  [exchange(): lax.all_to_all(blocks, axes, 0, 0, tiled=True, axis_index_groups=groups)]
    all_to_all x3, waiting for transfers between devices: 32.5 us -> 17.2 us  [exchange(): lax.all_to_all(blocks, axes, 0, 0, tiled=True, axis_index_groups=groups)]
    all_to_all x3, starting transfers between devices: 31.2 us -> 24.2 us  [exchange(): lax.all_to_all(blocks, axes, 0, 0, tiled=True, axis_index_groups=groups)]
    pallas_call x8 -> x10, Pallas kernels: 13.6 us -> 10.8 us  [call(): pl.pallas_call(kernel, out_shape=outs, in_specs=spec, out_specs=[pl.Block...]
    unnamed x21 -> x7, local copies, waits for them, and re-layouts: 4.97 us -> 2.39 us
  transfers between devices with their start and end apart: 3 -> 3, of which waited for: 3 -> 3; matrix products, arithmetic and copies ran while one was open for 0% -> 2% of each run, Pallas kernels for 3% -> 3%
where the time goes in v2:
time: 118 us; the launch traced here: 117 us
  blocking collectives  62.1 us (53%)
  starting transfers between devices  24.2 us (21%)
  waiting for transfers between devices  17.2 us (15%)
  Pallas kernels  10.8 us (9%)
  local copies, waits for them, and re-layouts  2.39 us (2%)
    all_to_all x4, blocking collectives, exchange(): lax.all_to_all(blocks, axes, 0, 0, tiled=True, axis_index_groups=groups)  62.1 us
    all_to_all x3, starting transfers between devices, exchange(): lax.all_to_all(blocks, axes, 0, 0, tiled=True, axis_index_groups=groups)  24.2 us
    all_to_all x3, waiting for transfers between devices, exchange(): lax.all_to_all(blocks, axes, 0, 0, tiled=True, axis_index_groups=groups)  17.2 us
    pallas_call x10, Pallas kernels, call(): pl.pallas_call(kernel, out_shape=outs, in_specs=spec, out_specs=[pl.Block...  10.8 us
    unnamed x7, local copies, waits for them, and re-layouts  2.39 us
  transfers between devices with their start and end apart: 3, of which 3 were waited for; matrix products, arithmetic and copies ran while one was open for 2% of the time, Pallas kernels for 3%

profile of v2, /device:TPU:1, one launch (start us, length us, event | category | flops | bytes accessed | tf_op | source)
XLA Modules:
  0.0 117.5 jit_solution(12034159177825199346)
XLA Ops:
  0.6 0.0 copy-start.1
  0.6 0.0 copy-start.2
  0.7 0.7 copy-done.1
  1.3 0.0 copy-done.2
  1.3 0.7 shard_map.58
  2.0 14.8 %all-to-all-start = ((f32[64,1,128]{2,1,0:T(1,128)}), f32[64,1,128]{2,1,0:T(1,128)S(1)}, u32[]{:S(2)}, u32[]{:S(2)}) async-start(f32[64,1,128]{2,1,0:T(1,128)} %bitcast.6), calls=%async_computation | async-start | bytes 65536 | tf_op jit(solution)/shard_map/all_to_all | solution.py:300
  16.8 0.0 copy-start
  16.9 1.7 %copy.10 = bf16[128,32,128]{2,0,1:T(8,128)(2,1)S(1)} copy(bf16[128,32,128]{2,1,0:T(8,128)(2,1)} %refs_2_.1) | data formatting | bytes 2097152 | tf_op args[0]
  18.6 0.1 pad_add_fusion.refs_0_
  18.7 7.5 %all-to-all-done = f32[64,1,128]{2,1,0:T(1,128)S(1)} async-done(((f32[64,1,128]{2,1,0:T(1,128)}), f32[64,1,128]{2,1,0:T(1,128)S(1)}, u32[]{:S(2)}, u32[]{:S(2)}) %all-to-all-start) | async-done | bytes 32800 | tf_op jit(solution)/shard_map/all_to_all | solution.py:300
  26.1 0.0 copy-done
  26.1 1.5 %shard_map.59 = f32[8,144,128]{2,1,0:T(8,128)S(1)} custom-call(s32[3]{0:T(128)S(1)} %pad_add_fusion.refs_0_, f32[64,128]{1,0:T(8,128)S(1)} %bitcast.16, bf16[128,32,128]{2,1,0:T(8,128)(2,1)S(1)} %copy-done), custom_call_target="tpu_custom_call" | custom-call | flops 67108864 | bytes 2719756 | tf_op jit(solution)/shard_map/pallas_call | solution.py:103
  27.6 24.2 %all_to_all.42.refs_0_ = f32[8,144,128]{2,1,0:T(8,128)S(1)} all-to-all(f32[8,144,128]{2,1,0:T(8,128)S(1)} %shard_map.59), channel_id=1, replica_groups=mesh['ia'=4,'ja'=16,'ka'=8] {'ka'}, dimensions={0} | all-to-all | bytes 1179648 | tf_op jit(solution)/shard_map/all_to_all | solution.py:300
  51.8 0.8 shard_map.60
  52.6 5.6 %all-to-all-start.2 = ((f32[16,8,128]{2,1,0:T(8,128)}), f32[16,8,128]{2,1,0:T(8,128)S(1)}, u32[]{:S(2)}, u32[]{:S(2)}) async-start(f32[16,8,128]{2,1,0:T(8,128)} %get-tuple-element.22), calls=%async_computation.2 | async-start | bytes 131072 | tf_op jit(solution)/shard_map/all_to_all | solution.py:300
  58.2 1.0 shard_map.61
  59.2 6.8 %all-to-all-done.2.refs_0_ = f32[16,8,128]{2,1,0:T(8,128)S(1)} async-done(((f32[16,8,128]{2,1,0:T(8,128)}), f32[16,8,128]{2,1,0:T(8,128)S(1)}, u32[]{:S(2)}, u32[]{:S(2)}) %all-to-all-start.2) | async-done | bytes 65568 | tf_op jit(solution)/shard_map/all_to_all | solution.py:300
  66.0 0.3 shard_map.62
  66.3 13.5 %all_to_all.43.refs_1_ = f32[32,12,128]{2,1,0:T(8,128)S(1)} all-to-all(f32[32,12,128]{2,1,0:T(8,128)S(1)} %shard_map.62), channel_id=1, replica_groups=mesh['ia'=4,'ja'=16,'ka'=8] {'ia','ka'}, dimensions={0} | all-to-all | bytes 393216 | tf_op jit(solution)/shard_map/all_to_all | solution.py:300
  79.8 2.5 %shard_map.63 = (f32[16,24,128]{2,1,0:T(8,128)S(1)}, f32[32,32]{1,0:T(8,128)S(1)}, f32[128,32]{1,0:T(8,128)S(1)}, f32[32,32]{1,0:T(8,128)S(1)}) custom-call(s32[3]{0:T(128)S(1)} %pad_add_fusion.refs_0_, f32[32,12,128]{2,1,0:T(8,128)S(1)} %all_to_all.43.refs_1_, f32[32,32]{1,0:T(8,128)S(1)} %get-tuple-element.26.refs_2_, bf16[32,128,128]{2,1,0:T(8,128)(2,1)S(1)} %bitcast.15), custom_call_target="tpu_custom_call" | custom-call | flops 67108864 | bytes 2519052 | tf_op jit(solution)/shard_map/pallas_call | solution.py:103
  82.3 14.8 %all_to_all.44.got_ref = f32[16,24,128]{2,1,0:T(8,128)S(1)} all-to-all(f32[16,24,128]{2,1,0:T(8,128)S(1)} %get-tuple-element.28), channel_id=1, replica_groups=mesh['ia'=4,'ja'=16,'ka'=8] {'ja'}, dimensions={0} | all-to-all | bytes 393216 | tf_op jit(solution)/shard_map/all_to_all | solution.py:300
  97.1 0.6 shard_map.64
  97.8 3.7 %all-to-all-start.5 = ((f32[8,16,128]{2,1,0:T(8,128)}), f32[8,16,128]{2,1,0:T(8,128)S(1)}, u32[]{:S(2)}, u32[]{:S(2)}) async-start(f32[8,16,128]{2,1,0:T(8,128)} %get-tuple-element.35), calls=%async_computation.5 | async-start | bytes 131072 | tf_op jit(solution)/shard_map/all_to_all | solution.py:300
  101.5 1.9 %shard_map.65 = (f32[32,32]{1,0:T(8,128)S(1)}, f32[1,32]{1,0:T(1,128)}, f32[1,32]{1,0:T(1,128)}) custom-call(s32[3]{0:T(128)S(1)} %pad_add_fusion.refs_0_, f32[8,128]{1,0:T(8,128)S(1)} %get-tuple-element.29.refs_1_, f32[32,32]{1,0:T(8,128)S(1)} %get-tuple-element.30.refs_2_, f32[128,32]{1,0:T(8,128)S(1)} %get-tuple-element.31.refs_3_, ...), custom_call_target="tpu_custom_call" | custom-call | flops 16777216 | bytes 33036 | tf_op jit(solution)/shard_map/pallas_call | solution.py:103
  103.5 2.9 %all-to-all-done.5.refs_1_ = f32[8,16,128]{2,1,0:T(8,128)S(1)} async-done(((f32[8,16,128]{2,1,0:T(8,128)}), f32[8,16,128]{2,1,0:T(8,128)S(1)}, u32[]{:S(2)}, u32[]{:S(2)}) %all-to-all-start.5) | async-done | bytes 65568 | tf_op jit(solution)/shard_map/all_to_all | solution.py:300
  106.4 0.8 shard_map.66
  107.2 9.7 %all_to_all.45.refs_0_ = f32[8,8,128]{2,1,0:T(8,128)S(1)} all-to-all(f32[8,8,128]{2,1,0:T(8,128)S(1)} %get-tuple-element.37), channel_id=1, replica_groups=mesh['ia'=4,'ja'=16,'ka'=8] {'ka'}, dimensions={0} | all-to-all | bytes 65536 | tf_op jit(solution)/shard_map/all_to_all | solution.py:300
  116.9 0.6 shard_map.67
Async XLA Ops:
  0.6 0.7 copy-start.1
  0.6 0.7 copy-start.2
  2.0 24.1 %all-to-all-start = ((f32[64,1,128]{2,1,0:T(1,128)}), f32[64,1,128]{2,1,0:T(1,128)S(1)}, u32[]{:S(2)}, u32[]{:S(2)}) async-start(f32[64,1,128]{2,1,0:T(1,128)} %bitcast.6), calls=%async_computation | async-start | bytes 65536 | tf_op jit(solution)/shard_map/all_to_all | solution.py:300
  16.8 9.3 %copy-start = (bf16[128,32,128]{2,1,0:T(8,128)(2,1)S(1)}, bf16[128,32,128]{2,1,0:T(8,128)(2,1)}, u32[]{:S(2)}) copy-start(bf16[128,32,128]{2,1,0:T(8,128)(2,1)} %refs_2_.1) | copy-start | bytes 3145732
  52.6 13.4 %all-to-all-start.2 = ((f32[16,8,128]{2,1,0:T(8,128)}), f32[16,8,128]{2,1,0:T(8,128)S(1)}, u32[]{:S(2)}, u32[]{:S(2)}) async-start(f32[16,8,128]{2,1,0:T(8,128)} %get-tuple-element.22), calls=%async_computation.2 | async-start | bytes 131072 | tf_op jit(solution)/shard_map/all_to_all | solution.py:300
  97.8 8.6 %all-to-all-start.5 = ((f32[8,16,128]{2,1,0:T(8,128)}), f32[8,16,128]{2,1,0:T(8,128)S(1)}, u32[]{:S(2)}, u32[]{:S(2)}) async-start(f32[8,16,128]{2,1,0:T(8,128)} %get-tuple-element.35), calls=%async_computation.5 | async-start | bytes 131072 | tf_op jit(solution)/shard_map/all_to_all | solution.py:300

commit v3 on v2

--- a/solution.py
+++ b/solution.py
@@ -96,7 +96,7 @@
     return row, column
 
 
-def call(kernel, outs, args, flops, scalars=0):
+def call(kernel, outs, args, flops, scalars=0, scratch=()):
     spec = [pl.BlockSpec(memory_space=pltpu.SMEM)] * scalars
     spec += [pl.BlockSpec(memory_space=pltpu.VMEM)] * (len(args) - scalars)
     moved = sum(4 * a.size for a in args) + sum(4 * o.size for o in outs)
@@ -105,6 +105,7 @@
         out_shape=outs,
         in_specs=spec,
         out_specs=[pl.BlockSpec(memory_space=pltpu.VMEM)] * len(outs),
+        scratch_shapes=[pltpu.VMEM(dims, F32) for dims in scratch],
         compiler_params=pltpu.CompilerParams(vmem_limit_bytes=24 * 2**20),
         cost_estimate=pl.CostEstimate(flops=flops, bytes_accessed=moved, transcendentals=0),
     )(*args)
@@ -171,7 +172,7 @@
         send_ref[ka, sums:, :] = riders
 
 
-def first_kernel(low_i, got_ref, send_ref, along_ref, grams_ref):
+def first_kernel(low_i, got_ref, send_ref, along_ref, weights_ref, gram_ref, grams_ref):
     sums = got_ref.shape[1] - 2 * SUB
     along = jnp.sum(got_ref[:, 0:sums, :], axis=0)
     along_ref[...] = along
@@ -187,9 +188,10 @@
         [jnp.sum(terms, axis=1), jnp.zeros((8 - low_i, LANES), F32)], axis=0
     )
     send_ref[...] = jnp.broadcast_to(summed[None], send_ref.shape)
-
-
-def weights_kernel(grams_ref, weights_ref, gram_ref):
+    first_weights(grams_ref, weights_ref, gram_ref)
+
+
+def first_weights(grams_ref, weights_ref, gram_ref):
     mixed = unpack(grams_ref[0:SUB])
     turned = mixed.T
     rows = lax.broadcasted_iota(jnp.int32, (R, R), 0)
@@ -213,27 +215,36 @@
     part = wide[:, 0:R]
     for g in range(1, PACK):
         part += wide[:, g * R : (g + 1) * R]
-    rows = jnp.concatenate([pack(part), solved], axis=0)
-    send_ref[...] = jnp.broadcast_to(rows[None], send_ref.shape)
+    rows = jnp.concatenate([pack(part), solved] * 2, axis=0)
+    for n in range(0, send_ref.shape[0], rows.shape[0]):
+        send_ref[n : n + rows.shape[0], :] = rows
 
 
 def third_kernel(
-    totals, sizes, place_ref, got_ref, gram_c_ref, turned_ref,
-    send_ref, gram_a_ref, factor_a_ref, solved_b_ref,
+    totals, sizes, low_i, place_ref, got_ref, gram_c_ref, turned_ref,
+    send_ref, gram_a_ref, factor_a_ref, solved_b_ref, everyone_ref,
 ):
     n_ia, n_ja, n_ka = sizes
     ia = place_ref[0]
-    peers, _, _ = got_ref.shape
-    low_i = got_ref.shape[1] - SUB
-    total = jnp.sum(got_ref[:, 0:SUB, :], axis=0)
-    everyone = jnp.concatenate([got_ref[n, SUB:, :] for n in range(peers)], axis=0)
+    each = SUB + low_i
+    pairs = got_ref.shape[0] // (2 * each)
+    summed = jnp.sum(got_ref[...].reshape(pairs, 2 * each, LANES), axis=0)
+    total = summed[0:SUB] + summed[each : each + SUB]
+    lower = lax.broadcasted_iota(jnp.int32, (2 * low_i, LANES), 0) < low_i
+    for n in range(pairs):
+        start = 2 * each * n
+        everyone_ref[2 * low_i * n : 2 * low_i * (n + 1), :] = jnp.where(
+            lower,
+            got_ref[start + SUB : start + 2 * SUB, :],
+            got_ref[start + 2 * SUB : start + 3 * SUB, :],
+        )
+    everyone = everyone_ref[...]
     gram_raw = lane_groups(dot(everyone, everyone, ((0,), (0,))))
     row, column = scales(gram_raw, totals[0])
     gram_a = gram_raw * row * column
     gram_a_ref[...] = gram_a
-    solved_a = unpack(
-        jnp.concatenate([got_ref[ia * n_ka + ka, SUB:, :] for ka in range(n_ka)], axis=0)
-    )
+    block = n_ka * low_i
+    solved_a = unpack(everyone_ref[pl.ds(pl.multiple_of(ia * block, block), block), :])
     factor_a = solved_a * row
     factor_a_ref[...] = factor_a
     summed = unpack(total) * row
@@ -324,23 +335,23 @@
         scalars=1,
     )
     got = exchange(send, "ka")
-    send, along, grams = call(
+    send, along, weights_a, gram_c = call(
         lambda *refs: first_kernel(low_i, *refs),
-        [shape(n_ja, 8, LANES), shape(low_i * rows_j, LANES), shape(2 * SUB, LANES)],
+        [shape(n_ja, 8, LANES), shape(low_i * rows_j, LANES), shape(LANES, LANES), shape(R, R)],
         [got],
         2**20,
+        scratch=[(2 * SUB, LANES)],
     )
     got = exchange(send, "ja")
-    weights_a, gram_c = call(weights_kernel, [shape(LANES, LANES), shape(R, R)], [grams], 2**24)
     (send,) = call(
         lambda *refs: second_kernel(low_i, *refs),
-        [shape(n_ia * n_ka, SUB + low_i, LANES)],
+        [shape(n_ia * n_ka * (SUB + low_i), LANES)],
         [got, weights_a, along],
         2**20,
     )
-    got = exchange(send, ("ia", "ka"))
+    got = exchange(send[:, None, :], ("ia", "ka"))[:, 0, :]
     send, gram_a, factor_a, solved_b = call(
-        lambda *refs: third_kernel(totals, sizes, *refs),
+        lambda *refs: third_kernel(totals, sizes, low_i, *refs),
         [
             shape(n_ja, R // 2 + SUB, LANES),
             shape(R, R),
@@ -350,6 +361,7 @@
         [place, got, gram_c, turned],
         2**26,
         scalars=1,
+        scratch=[(n_ia * n_ka * low_i, LANES)],
     )
     got = exchange(send, "ja")
     send, gram_b = call(

time: 118 us -> 116 us (0.983)
  blocking collectives: 62.1 us -> 73.6 us
  waiting for transfers between devices: 17.2 us -> 10.4 us
  starting transfers between devices: 24.2 us -> 18.2 us
    all_to_all x4 -> x5, blocking collectives: 62.1 us -> 73.6 us  [exchange(): lax.all_to_all(blocks, axes, 0, 0, tiled=True, axis_index_groups=groups)]
    all_to_all x3 -> x2, waiting for transfers between devices: 17.2 us -> 10.4 us  [exchange(): lax.all_to_all(blocks, axes, 0, 0, tiled=True, axis_index_groups=groups)]
    all_to_all x3 -> x2, starting transfers between devices: 24.2 us -> 18.2 us  [exchange(): lax.all_to_all(blocks, axes, 0, 0, tiled=True, axis_index_groups=groups)]
    pallas_call x10 -> x9, Pallas kernels: 10.8 us -> 10.1 us  [call(): pl.pallas_call(kernel, out_shape=outs, in_specs=spec, out_specs=[pl.Block...]
  transfers between devices with their start and end apart: 3 -> 2, of which waited for: 3 -> 2; matrix products, arithmetic and copies ran while one was open for 2% -> 2% of each run, Pallas kernels for 3% -> 2%
where the time goes in v3:
time: 116 us; the launch traced here: 115 us
  blocking collectives  73.6 us (63%)
  starting transfers between devices  18.2 us (16%)
  waiting for transfers between devices  10.4 us (9%)
  Pallas kernels  10.1 us (9%)
  local copies, waits for them, and re-layouts  2.39 us (2%)
    all_to_all x5, blocking collectives, exchange(): lax.all_to_all(blocks, axes, 0, 0, tiled=True, axis_index_groups=groups)  73.6 us
    all_to_all x2, starting transfers between devices, exchange(): lax.all_to_all(blocks, axes, 0, 0, tiled=True, axis_index_groups=groups)  18.2 us
    all_to_all x2, waiting for transfers between devices, exchange(): lax.all_to_all(blocks, axes, 0, 0, tiled=True, axis_index_groups=groups)  10.4 us
    pallas_call x9, Pallas kernels, call(): pl.pallas_call(kernel, out_shape=outs, in_specs=spec, out_specs=[pl.Block...  10.1 us
    unnamed x7, local copies, waits for them, and re-layouts  2.39 us
  transfers between devices with their start and end apart: 2, of which 2 were waited for; matrix products, arithmetic and copies ran while one was open for 2% of the time, Pallas kernels for 2%

profile of v3, /device:TPU:1, one launch (start us, length us, event | category | flops | bytes accessed | tf_op | source)
XLA Modules:
  0.0 115.5 jit_solution(8280193508860050840)
XLA Ops:
  0.6 0.0 copy-start.1
  0.6 0.0 copy-start.2
  0.7 0.7 copy-done.1
  1.3 0.0 copy-done.2
  1.3 0.7 shard_map.58
  2.0 14.8 %all-to-all-start = ((f32[64,1,128]{2,1,0:T(1,128)}), f32[64,1,128]{2,1,0:T(1,128)S(1)}, u32[]{:S(2)}, u32[]{:S(2)}) async-start(f32[64,1,128]{2,1,0:T(1,128)} %bitcast.6), calls=%async_computation | async-start | bytes 65536 | tf_op jit(solution)/shard_map/all_to_all | solution.py:311
  16.8 0.0 copy-start
  16.8 1.7 %copy.11 = bf16[128,32,128]{2,0,1:T(8,128)(2,1)S(1)} copy(bf16[128,32,128]{2,1,0:T(8,128)(2,1)} %refs_2_.1) | data formatting | bytes 2097152 | tf_op args[0]
  18.6 0.1 pad_add_fusion.refs_0_
  18.7 7.5 %all-to-all-done = f32[64,1,128]{2,1,0:T(1,128)S(1)} async-done(((f32[64,1,128]{2,1,0:T(1,128)}), f32[64,1,128]{2,1,0:T(1,128)S(1)}, u32[]{:S(2)}, u32[]{:S(2)}) %all-to-all-start) | async-done | bytes 32800 | tf_op jit(solution)/shard_map/all_to_all | solution.py:311
  26.1 0.0 copy-done
  26.1 1.5 %shard_map.59 = f32[8,144,128]{2,1,0:T(8,128)S(1)} custom-call(s32[3]{0:T(128)S(1)} %pad_add_fusion.refs_0_, f32[64,128]{1,0:T(8,128)S(1)} %bitcast.22, bf16[128,32,128]{2,1,0:T(8,128)(2,1)S(1)} %copy-done), custom_call_target="tpu_custom_call" | custom-call | flops 67108864 | bytes 2719756 | tf_op jit(solution)/shard_map/pallas_call | solution.py:103
  27.6 24.1 %all_to_all.42.refs_0_ = f32[8,144,128]{2,1,0:T(8,128)S(1)} all-to-all(f32[8,144,128]{2,1,0:T(8,128)S(1)} %shard_map.59), channel_id=1, replica_groups=mesh['ia'=4,'ja'=16,'ka'=8] {'ka'}, dimensions={0} | all-to-all | bytes 1179648 | tf_op jit(solution)/shard_map/all_to_all | solution.py:311
  51.7 1.0 shard_map.60
  52.7 12.6 %all_to_all.43.refs_0_ = f32[16,8,128]{2,1,0:T(8,128)S(1)} all-to-all(f32[16,8,128]{2,1,0:T(8,128)S(1)} %get-tuple-element.21), channel_id=1, replica_groups=mesh['ia'=4,'ja'=16,'ka'=8] {'ja'}, dimensions={0} | all-to-all | bytes 131072 | tf_op jit(solution)/shard_map/all_to_all | solution.py:311
  65.3 0.3 shard_map.61
  65.7 12.9 %all_to_all.44 = f32[384,1,128]{2,1,0:T(1,128)S(1)} all-to-all(f32[384,1,128]{2,1,0:T(1,128)S(1)} %bitcast.21), channel_id=1, replica_groups=mesh['ia'=4,'ja'=16,'ka'=8] {'ia','ka'}, dimensions={0} | all-to-all | bytes 393216 | tf_op jit(solution)/shard_map/all_to_all | solution.py:311
  78.6 2.5 %shard_map.62 = (f32[16,24,128]{2,1,0:T(8,128)S(1)}, f32[32,32]{1,0:T(8,128)S(1)}, f32[128,32]{1,0:T(8,128)S(1)}, f32[32,32]{1,0:T(8,128)S(1)}) custom-call(s32[3]{0:T(128)S(1)} %pad_add_fusion.refs_0_, f32[384,128]{1,0:T(8,128)S(1)} %bitcast.20, f32[32,32]{1,0:T(8,128)S(1)} %get-tuple-element.24.refs_2_, bf16[32,128,128]{2,1,0:T(8,128)(2,1)S(1)} %bitcast.19), custom_call_target="tpu_custom_call" | custom-call | flops 67108864 | bytes 2519052 | tf_op jit(solution)/shard_map/pallas_call | solution.py:103
  81.1 14.8 %all_to_all.45.got_ref = f32[16,24,128]{2,1,0:T(8,128)S(1)} all-to-all(f32[16,24,128]{2,1,0:T(8,128)S(1)} %get-tuple-element.26), channel_id=1, replica_groups=mesh['ia'=4,'ja'=16,'ka'=8] {'ja'}, dimensions={0} | all-to-all | bytes 393216 | tf_op jit(solution)/shard_map/all_to_all | solution.py:311
  95.9 0.6 shard_map.63
  96.5 3.4 %all-to-all-start.5 = ((f32[8,16,128]{2,1,0:T(8,128)}), f32[8,16,128]{2,1,0:T(8,128)S(1)}, u32[]{:S(2)}, u32[]{:S(2)}) async-start(f32[8,16,128]{2,1,0:T(8,128)} %get-tuple-element.33), calls=%async_computation.5 | async-start | bytes 131072 | tf_op jit(solution)/shard_map/all_to_all | solution.py:311
  99.9 1.9 %shard_map.64 = (f32[32,32]{1,0:T(8,128)S(1)}, f32[1,32]{1,0:T(1,128)}, f32[1,32]{1,0:T(1,128)}) custom-call(s32[3]{0:T(128)S(1)} %pad_add_fusion.refs_0_, f32[8,128]{1,0:T(8,128)S(1)} %get-tuple-element.27.refs_1_, f32[32,32]{1,0:T(8,128)S(1)} %get-tuple-element.28.refs_2_, f32[128,32]{1,0:T(8,128)S(1)} %get-tuple-element.29.refs_3_, ...), custom_call_target="tpu_custom_call" | custom-call | flops 16777216 | bytes 33036 | tf_op jit(solution)/shard_map/pallas_call | solution.py:103
  101.9 2.9 %all-to-all-done.5.refs_1_ = f32[8,16,128]{2,1,0:T(8,128)S(1)} async-done(((f32[8,16,128]{2,1,0:T(8,128)}), f32[8,16,128]{2,1,0:T(8,128)S(1)}, u32[]{:S(2)}, u32[]{:S(2)}) %all-to-all-start.5) | async-done | bytes 65568 | tf_op jit(solution)/shard_map/all_to_all | solution.py:311
  104.8 0.8 shard_map.65
  105.6 9.3 %all_to_all.46.refs_0_ = f32[8,8,128]{2,1,0:T(8,128)S(1)} all-to-all(f32[8,8,128]{2,1,0:T(8,128)S(1)} %get-tuple-element.35), channel_id=1, replica_groups=mesh['ia'=4,'ja'=16,'ka'=8] {'ka'}, dimensions={0} | all-to-all | bytes 65536 | tf_op jit(solution)/shard_map/all_to_all | solution.py:311
  114.9 0.6 shard_map.66
Async XLA Ops:
  0.6 0.7 copy-start.1
  0.6 0.7 copy-start.2
  2.0 24.1 %all-to-all-start = ((f32[64,1,128]{2,1,0:T(1,128)}), f32[64,1,128]{2,1,0:T(1,128)S(1)}, u32[]{:S(2)}, u32[]{:S(2)}) async-start(f32[64,1,128]{2,1,0:T(1,128)} %bitcast.6), calls=%async_computation | async-start | bytes 65536 | tf_op jit(solution)/shard_map/all_to_all | solution.py:311
  16.8 9.3 %copy-start = (bf16[128,32,128]{2,1,0:T(8,128)(2,1)S(1)}, bf16[128,32,128]{2,1,0:T(8,128)(2,1)}, u32[]{:S(2)}) copy-start(bf16[128,32,128]{2,1,0:T(8,128)(2,1)} %refs_2_.1) | copy-start | bytes 3145732
  96.5 8.3 %all-to-all-start.5 = ((f32[8,16,128]{2,1,0:T(8,128)}), f32[8,16,128]{2,1,0:T(8,128)S(1)}, u32[]{:S(2)}, u32[]{:S(2)}) async-start(f32[8,16,128]{2,1,0:T(8,128)} %get-tuple-element.33), calls=%async_computation.5 | async-start | bytes 131072 | tf_op jit(solution)/shard_map/all_to_all | solution.py:311

commit v4 on v3

--- a/solution.py
+++ b/solution.py
@@ -140,17 +140,17 @@
     weights = jnp.concatenate(
         [jnp.where(lane == g, tiled, 0.0).astype(BF16) for g in range(PACK)], axis=0
     )
-    low_i = rows_i // (PACK * n_ka)
-    sums = low_i * rows_j
-    for ka in range(n_ka):
-        left = jnp.concatenate(
-            [
-                tensor_ref[(g * n_ka + ka) * low_i : (g * n_ka + ka + 1) * low_i].reshape(sums, rows_k)
-                for g in range(PACK)
-            ],
-            axis=1,
-        )
-        send_ref[ka, 0:sums, :] = jnp.dot(left, weights, preferred_element_type=F32)
+    group_i = rows_i // PACK
+    sums = group_i // n_ka * rows_j
+    left = jnp.concatenate(
+        [
+            tensor_ref[g * group_i : (g + 1) * group_i].reshape(group_i * rows_j, rows_k)
+            for g in range(PACK)
+        ],
+        axis=1,
+    )
+    product = jnp.dot(left, weights, preferred_element_type=F32)
+    send_ref[:, 0:sums, :] = product.reshape(n_ka, sums, LANES)
     products = dot(rows, rows, ((0,), (0,)))
     gram_b = products[0:R, 0:R]
     gram_c = products[R : 2 * R, R : 2 * R] + products[2 * R : 3 * R, 2 * R : 3 * R]
@@ -247,16 +247,19 @@
     solved_a = unpack(everyone_ref[pl.ds(pl.multiple_of(ia * block, block), block), :])
     factor_a = solved_a * row
     factor_a_ref[...] = factor_a
-    summed = unpack(total) * row
-    solved_b = dot(summed, unpack(inverse(pack(gram_a * gram_c_ref[...]))))
+    summed = (unpack(total) * row).T
+    solved_b = dot(unpack(inverse(pack(gram_a * gram_c_ref[...]))), summed)
     solved_b_ref[...] = solved_b
-    gram_b = pack(dot(solved_b, solved_b, ((0,), (0,))))
+    gram_b = pack(dot(solved_b, solved_b, ((1,), (1,))))
     a_low = factor_a.astype(BF16).T
-    b_turned = solved_b.T
     part = jnp.zeros((R, turned_ref.shape[2]), F32)
-    for j in range(turned_ref.shape[0]):
-        along = jnp.dot(a_low, turned_ref[j], preferred_element_type=F32)
-        part += along * b_turned[:, j : j + 1]
+    rows_j, rows_k = turned_ref.shape[0], turned_ref.shape[2]
+    step = 8
+    for start in range(0, rows_j, step):
+        right = jnp.concatenate([turned_ref[start + j] for j in range(step)], axis=1)
+        along = jnp.dot(a_low, right, preferred_element_type=F32)
+        for j in range(step):
+            part += along[:, j * rows_k : (j + 1) * rows_k] * solved_b[:, start + j : start + j + 1]
     half = R // 2
     first = jnp.concatenate([part[:half], gram_b], axis=0)
     second = jnp.concatenate([part[half:], gram_b], axis=0)
@@ -280,11 +283,14 @@
     row, column = scales(gram_raw, totals[1])
     gram_b = gram_raw * row * column
     out_a_ref[...] = factor_a_ref[pl.ds(ja * n_ka + ka, 1), :]
-    out_b_ref[...] = solved_b_ref[pl.ds(ia * n_ka + ka, 1), :] * row
-    weights_ref[...] = unpack(inverse(pack(gram_a_ref[...] * gram_b))) * row
-
-
-def fourth_kernel(sizes, place_ref, got_ref, weights_ref, send_ref, own_c_ref):
+    solved_b = solved_b_ref[...]
+    j_of = lax.broadcasted_iota(jnp.int32, (8, solved_b.shape[1]), 1)
+    chosen = jnp.where(j_of == ia * n_ka + ka, 1.0, 0.0)
+    out_b_ref[...] = dot(chosen, solved_b, ((1,), (1,)))[0:1] * row
+    weights_ref[...] = unpack(inverse(pack(gram_a_ref[...] * gram_b))) * column
+
+
+def fourth_kernel(sizes, place_ref, got_ref, weights_ref, send_ref, own_c_ref, solved_ref):
     n_ia, n_ja, n_ka = sizes
     ia, ja = place_ref[0], place_ref[1]
     first = got_ref[0]
@@ -292,19 +298,20 @@
     for n in range(1, n_ia):
         first += got_ref[2 * n]
         second += got_ref[2 * n + 1]
-    solved = dot(weights_ref[...], jnp.concatenate([first, second], axis=0))
-    squares = dot(jnp.ones((8, solved.shape[1]), F32), solved * solved, ((1,), (1,)))
-    squares = jnp.concatenate([squares, jnp.zeros((8, LANES - R), F32)], axis=1)
+    solved = dot(jnp.concatenate([first, second], axis=0).T, weights_ref[...])
+    solved_ref[...] = solved
+    squares = jnp.sum(solved * solved, axis=0, keepdims=True)
+    squares = jnp.concatenate([squares, jnp.zeros((1, LANES - R), F32)], axis=1)
     send_ref[...] = jnp.broadcast_to(squares[None], send_ref.shape)
-    k_of = lax.broadcasted_iota(jnp.int32, (8, solved.shape[1]), 1)
-    t_of = lax.broadcasted_iota(jnp.int32, (8, solved.shape[1]), 0)
-    chosen = jnp.where(k_of == 2 * (ia * n_ja + ja) + t_of, 1.0, 0.0)
-    own_c_ref[...] = dot(chosen, solved, ((1,), (1,)))
+    own = 2 * (ia * n_ja + ja)
+    own_c_ref[...] = jnp.concatenate(
+        [solved_ref[pl.ds(own, 1), :], solved_ref[pl.ds(own + 1, 1), :]], axis=0
+    )
 
 
 def last_kernel(total, got_ref, own_c_ref, out_ref):
     squares = jnp.sum(got_ref[...], axis=0)[0:1, 0:R]
-    out_ref[...] = own_c_ref[0:2, :] * lax.rsqrt(squares / total + 1e-06)
+    out_ref[...] = own_c_ref[...] * lax.rsqrt(squares / total + 1e-06)
 
 
 def exchange(blocks, axes, groups=None):
@@ -356,7 +363,7 @@
             shape(n_ja, R // 2 + SUB, LANES),
             shape(R, R),
             shape(rows_i, R),
-            shape(rows_j, R),
+            shape(R, rows_j),
         ],
         [place, got, gram_c, turned],
         2**26,
@@ -377,10 +384,11 @@
     )
     send, own_c = call(
         lambda *refs: fourth_kernel(sizes, *refs),
-        [shape(n_ka, 8, LANES), shape(8, R)],
+        [shape(n_ka, 8, LANES), shape(2, R)],
         [place, got, weights_c],
         2**20,
         scalars=1,
+        scratch=[(rows_k, R)],
     )
     got = exchange(send, "ka")
     (out_c,) = call(

time: 116 us -> 116 us (level)
  no operation moved by 1% of the time
where the time goes in v4:
time: 116 us; the launch traced here: 115 us
  blocking collectives  73.6 us (63%)
  starting transfers between devices  18.2 us (16%)
  waiting for transfers between devices  10.4 us (9%)
  Pallas kernels  9.8 us (8%)
  local copies, waits for them, and re-layouts  2.39 us (2%)
    all_to_all x5, blocking collectives, exchange(): lax.all_to_all(blocks, axes, 0, 0, tiled=True, axis_index_groups=groups)  73.6 us
    all_to_all x2, starting transfers between devices, exchange(): lax.all_to_all(blocks, axes, 0, 0, tiled=True, axis_index_groups=groups)  18.2 us
    all_to_all x2, waiting for transfers between devices, exchange(): lax.all_to_all(blocks, axes, 0, 0, tiled=True, axis_index_groups=groups)  10.4 us
    pallas_call x9, Pallas kernels, call(): pl.pallas_call(kernel, out_shape=outs, in_specs=spec, out_specs=[pl.Block...  9.8 us
    unnamed x7, local copies, waits for them, and re-layouts  2.39 us
  transfers between devices with their start and end apart: 2, of which 2 were waited for; matrix products, arithmetic and copies ran while one was open for 2% of the time, Pallas kernels for 2%

profile of v4, /device:TPU:1, one launch (start us, length us, event | category | flops | bytes accessed | tf_op | source)
XLA Modules:
  0.0 115.2 jit_solution(1395008676056689579)
XLA Ops:
  0.6 0.0 copy-start.1
  0.6 0.0 copy-start.2
  0.7 0.7 copy-done.1
  1.3 0.0 copy-done.2
  1.3 0.7 shard_map.58
  2.0 14.8 %all-to-all-start = ((f32[64,1,128]{2,1,0:T(1,128)}), f32[64,1,128]{2,1,0:T(1,128)S(1)}, u32[]{:S(2)}, u32[]{:S(2)}) async-start(f32[64,1,128]{2,1,0:T(1,128)} %bitcast.6), calls=%async_computation | async-start | bytes 65536 | tf_op jit(solution)/shard_map/all_to_all | solution.py:318
  16.8 0.0 copy-start
  16.8 1.7 %copy.11 = bf16[128,32,128]{2,0,1:T(8,128)(2,1)S(1)} copy(bf16[128,32,128]{2,1,0:T(8,128)(2,1)} %refs_2_.1) | data formatting | bytes 2097152 | tf_op args[0]
  18.6 0.1 pad_add_fusion.refs_0_
  18.7 7.5 %all-to-all-done = f32[64,1,128]{2,1,0:T(1,128)S(1)} async-done(((f32[64,1,128]{2,1,0:T(1,128)}), f32[64,1,128]{2,1,0:T(1,128)S(1)}, u32[]{:S(2)}, u32[]{:S(2)}) %all-to-all-start) | async-done | bytes 32800 | tf_op jit(solution)/shard_map/all_to_all | solution.py:318
  26.1 0.0 copy-done
  26.1 1.5 %shard_map.59 = f32[8,144,128]{2,1,0:T(8,128)S(1)} custom-call(s32[3]{0:T(128)S(1)} %pad_add_fusion.refs_0_, f32[64,128]{1,0:T(8,128)S(1)} %bitcast.22, bf16[128,32,128]{2,1,0:T(8,128)(2,1)S(1)} %copy-done), custom_call_target="tpu_custom_call" | custom-call | flops 67108864 | bytes 2719756 | tf_op jit(solution)/shard_map/pallas_call | solution.py:103
  27.6 24.1 %all_to_all.42.refs_0_ = f32[8,144,128]{2,1,0:T(8,128)S(1)} all-to-all(f32[8,144,128]{2,1,0:T(8,128)S(1)} %shard_map.59), channel_id=1, replica_groups=mesh['ia'=4,'ja'=16,'ka'=8] {'ka'}, dimensions={0} | all-to-all | bytes 1179648 | tf_op jit(solution)/shard_map/all_to_all | solution.py:318
  51.8 1.0 shard_map.60
  52.8 12.6 %all_to_all.43.refs_0_ = f32[16,8,128]{2,1,0:T(8,128)S(1)} all-to-all(f32[16,8,128]{2,1,0:T(8,128)S(1)} %get-tuple-element.21), channel_id=1, replica_groups=mesh['ia'=4,'ja'=16,'ka'=8] {'ja'}, dimensions={0} | all-to-all | bytes 131072 | tf_op jit(solution)/shard_map/all_to_all | solution.py:318
  65.3 0.3 shard_map.61
  65.7 12.9 %all_to_all.44 = f32[384,1,128]{2,1,0:T(1,128)S(1)} all-to-all(f32[384,1,128]{2,1,0:T(1,128)S(1)} %bitcast.21), channel_id=1, replica_groups=mesh['ia'=4,'ja'=16,'ka'=8] {'ia','ka'}, dimensions={0} | all-to-all | bytes 393216 | tf_op jit(solution)/shard_map/all_to_all | solution.py:318
  78.6 2.3 %shard_map.62 = (f32[16,24,128]{2,1,0:T(8,128)S(1)}, f32[32,32]{1,0:T(8,128)S(1)}, f32[128,32]{1,0:T(8,128)S(1)}, f32[32,32]{1,0:T(8,128)S(1)}) custom-call(s32[3]{0:T(128)S(1)} %pad_add_fusion.refs_0_, f32[384,128]{1,0:T(8,128)S(1)} %bitcast.20, f32[32,32]{1,0:T(8,128)S(1)} %get-tuple-element.24.refs_2_, bf16[32,128,128]{2,1,0:T(8,128)(2,1)S(1)} %bitcast.19), custom_call_target="tpu_custom_call" | custom-call | flops 67108864 | bytes 2519052 | tf_op jit(solution)/shard_map/pallas_call | solution.py:103
  80.9 14.8 %all_to_all.45.got_ref = f32[16,24,128]{2,1,0:T(8,128)S(1)} all-to-all(f32[16,24,128]{2,1,0:T(8,128)S(1)} %get-tuple-element.26), channel_id=1, replica_groups=mesh['ia'=4,'ja'=16,'ka'=8] {'ja'}, dimensions={0} | all-to-all | bytes 393216 | tf_op jit(solution)/shard_map/all_to_all | solution.py:318
  95.7 0.6 shard_map.63
  96.3 3.4 %all-to-all-start.5 = ((f32[8,16,128]{2,1,0:T(8,128)}), f32[8,16,128]{2,1,0:T(8,128)S(1)}, u32[]{:S(2)}, u32[]{:S(2)}) async-start(f32[8,16,128]{2,1,0:T(8,128)} %get-tuple-element.33), calls=%async_computation.5 | async-start | bytes 131072 | tf_op jit(solution)/shard_map/all_to_all | solution.py:318
  99.7 1.9 %shard_map.64 = (f32[32,32]{1,0:T(8,128)S(1)}, f32[1,32]{1,0:T(1,128)}, f32[1,32]{1,0:T(1,128)}) custom-call(s32[3]{0:T(128)S(1)} %pad_add_fusion.refs_0_, f32[8,128]{1,0:T(8,128)S(1)} %get-tuple-element.27.refs_1_, f32[32,32]{1,0:T(8,128)S(1)} %get-tuple-element.28.refs_2_, f32[128,32]{1,0:T(8,128)S(1)} %get-tuple-element.29.refs_3_, ...), custom_call_target="tpu_custom_call" | custom-call | flops 16777216 | bytes 33036 | tf_op jit(solution)/shard_map/pallas_call | solution.py:103
  101.7 2.9 %all-to-all-done.5.refs_1_ = f32[8,16,128]{2,1,0:T(8,128)S(1)} async-done(((f32[8,16,128]{2,1,0:T(8,128)}), f32[8,16,128]{2,1,0:T(8,128)S(1)}, u32[]{:S(2)}, u32[]{:S(2)}) %all-to-all-start.5) | async-done | bytes 65568 | tf_op jit(solution)/shard_map/all_to_all | solution.py:318
  104.6 0.8 shard_map.65
  105.4 9.2 %all_to_all.46.refs_0_ = f32[8,8,128]{2,1,0:T(8,128)S(1)} all-to-all(f32[8,8,128]{2,1,0:T(8,128)S(1)} %get-tuple-element.35), channel_id=1, replica_groups=mesh['ia'=4,'ja'=16,'ka'=8] {'ka'}, dimensions={0} | all-to-all | bytes 65536 | tf_op jit(solution)/shard_map/all_to_all | solution.py:318
  114.6 0.6 shard_map.66
Async XLA Ops:
  0.6 0.7 copy-start.1
  0.6 0.7 copy-start.2
  2.0 24.1 %all-to-all-start = ((f32[64,1,128]{2,1,0:T(1,128)}), f32[64,1,128]{2,1,0:T(1,128)S(1)}, u32[]{:S(2)}, u32[]{:S(2)}) async-start(f32[64,1,128]{2,1,0:T(1,128)} %bitcast.6), calls=%async_computation | async-start | bytes 65536 | tf_op jit(solution)/shard_map/all_to_all | solution.py:318
  16.8 9.3 %copy-start = (bf16[128,32,128]{2,1,0:T(8,128)(2,1)S(1)}, bf16[128,32,128]{2,1,0:T(8,128)(2,1)}, u32[]{:S(2)}) copy-start(bf16[128,32,128]{2,1,0:T(8,128)(2,1)} %refs_2_.1) | copy-start | bytes 3145732
  96.3 8.3 %all-to-all-start.5 = ((f32[8,16,128]{2,1,0:T(8,128)}), f32[8,16,128]{2,1,0:T(8,128)S(1)}, u32[]{:S(2)}, u32[]{:S(2)}) async-start(f32[8,16,128]{2,1,0:T(8,128)} %get-tuple-element.33), calls=%async_computation.5 | async-start | bytes 131072 | tf_op jit(solution)/shard_map/all_to_all | solution.py:318

commit v5 on v4

--- a/solution.py
+++ b/solution.py
@@ -150,7 +150,7 @@
         axis=1,
     )
     product = jnp.dot(left, weights, preferred_element_type=F32)
-    send_ref[:, 0:sums, :] = product.reshape(n_ka, sums, LANES)
+    send_ref[:, 0:sums, :] = product.astype(BF16).reshape(n_ka, sums, LANES)
     products = dot(rows, rows, ((0,), (0,)))
     gram_b = products[0:R, 0:R]
     gram_c = products[R : 2 * R, R : 2 * R] + products[2 * R : 3 * R, 2 * R : 3 * R]
@@ -164,22 +164,33 @@
             pack(jnp.where(upper, gram_b, gram_c)),
             own_b,
             jnp.concatenate([diagonal, jnp.zeros((1, LANES - R), F32)], axis=1),
-            jnp.zeros((SUB - 2, LANES), F32),
         ],
         axis=0,
     )
+    high = riders.astype(BF16).astype(F32)
+    middle = (riders - high).astype(BF16).astype(F32)
+    low = riders - high - middle
+    riders = jnp.concatenate([high, middle, low, jnp.zeros((2, LANES), F32)], axis=0).astype(BF16)
     for ka in range(n_ka):
         send_ref[ka, sums:, :] = riders
 
 
 def first_kernel(low_i, got_ref, send_ref, along_ref, weights_ref, gram_ref, grams_ref):
-    sums = got_ref.shape[1] - 2 * SUB
-    along = jnp.sum(got_ref[:, 0:sums, :], axis=0)
+    sums = got_ref.shape[1] - 4 * SUB
+    n_ka = got_ref.shape[0]
+    along = jnp.zeros((sums, LANES), F32)
+    own_b = []
+    total = jnp.zeros((SUB + 2, LANES), F32)
+    for ka in range(n_ka):
+        along += got_ref[ka, 0:sums, :].astype(F32)
+        parts = got_ref[ka, sums:, :].astype(F32)
+        size = SUB + 2
+        riders = (parts[0:size] + parts[size : 2 * size]) + parts[2 * size : 3 * size]
+        total += riders
+        own_b.append(riders[SUB : SUB + 1])
     along_ref[...] = along
-    grams_ref[...] = jnp.sum(got_ref[:, sums:, :], axis=0)
-    own_b = jnp.concatenate(
-        [got_ref[ka, sums + SUB : sums + SUB + 1, :] for ka in range(got_ref.shape[0])], axis=0
-    )
+    grams_ref[...] = jnp.concatenate([total, jnp.zeros((SUB - 2, LANES), F32)], axis=0)
+    own_b = jnp.concatenate(own_b, axis=0)
     block_b = unpack(own_b)
     rows_j = block_b.shape[0]
     wide_b = jnp.concatenate([block_b] * PACK, axis=1)
@@ -336,7 +347,7 @@
     rows, turned = lax.optimization_barrier((rows, turned))
     (send,) = call(
         lambda *refs: along_kernel(sizes, *refs),
-        [shape(n_ka, low_i * rows_j + 2 * SUB, LANES)],
+        [shape(n_ka, low_i * rows_j + 4 * SUB, LANES, dtype=BF16)],
         [place, rows, tensor],
         2**26,
         scalars=1,

time: 116 us -> 110 us (0.948)
  blocking collectives: 73.6 us -> 68 us
    all_to_all x5, blocking collectives: 73.6 us -> 68 us  [exchange(): lax.all_to_all(blocks, axes, 0, 0, tiled=True, axis_index_groups=groups)]
where the time goes in v5:
time: 110 us
  blocking collectives  68 us (62%)
  starting transfers between devices  18.2 us (17%)
  waiting for transfers between devices  10.4 us (9%)
  Pallas kernels  9.82 us (9%)
  local copies, waits for them, and re-layouts  2.39 us (2%)
    all_to_all x5, blocking collectives, exchange(): lax.all_to_all(blocks, axes, 0, 0, tiled=True, axis_index_groups=groups)  68 us
    all_to_all x2, starting transfers between devices, exchange(): lax.all_to_all(blocks, axes, 0, 0, tiled=True, axis_index_groups=groups)  18.2 us
    all_to_all x2, waiting for transfers between devices, exchange(): lax.all_to_all(blocks, axes, 0, 0, tiled=True, axis_index_groups=groups)  10.4 us
    pallas_call x9, Pallas kernels, call(): pl.pallas_call(kernel, out_shape=outs, in_specs=spec, out_specs=[pl.Block...  9.82 us
    unnamed x7, local copies, waits for them, and re-layouts  2.39 us
  transfers between devices with their start and end apart: 2, of which 2 were waited for; matrix products, arithmetic and copies ran while one was open for 2% of the time, Pallas kernels for 2%

profile of v5, /device:TPU:1, one launch (start us, length us, event | category | flops | bytes accessed | tf_op | source)
XLA Modules:
  0.0 109.6 jit_solution(12813783189152018984)
XLA Ops:
  0.6 0.0 copy-start.1
  0.6 0.0 copy-start.2
  0.7 0.7 copy-done.1
  1.3 0.0 copy-done.2
  1.3 0.7 shard_map.58
  2.0 14.8 %all-to-all-start = ((f32[64,1,128]{2,1,0:T(1,128)}), f32[64,1,128]{2,1,0:T(1,128)S(1)}, u32[]{:S(2)}, u32[]{:S(2)}) async-start(f32[64,1,128]{2,1,0:T(1,128)} %bitcast.6), calls=%async_computation | async-start | bytes 65536 | tf_op jit(solution)/shard_map/all_to_all | solution.py:329
  16.8 0.0 copy-start
  16.8 1.7 %copy.11 = bf16[128,32,128]{2,0,1:T(8,128)(2,1)S(1)} copy(bf16[128,32,128]{2,1,0:T(8,128)(2,1)} %refs_2_.1) | data formatting | bytes 2097152 | tf_op args[0]
  18.6 0.1 pad_add_fusion.refs_0_
  18.7 7.5 %all-to-all-done = f32[64,1,128]{2,1,0:T(1,128)S(1)} async-done(((f32[64,1,128]{2,1,0:T(1,128)}), f32[64,1,128]{2,1,0:T(1,128)S(1)}, u32[]{:S(2)}, u32[]{:S(2)}) %all-to-all-start) | async-done | bytes 32800 | tf_op jit(solution)/shard_map/all_to_all | solution.py:329
  26.1 0.0 copy-done
  26.1 1.5 %shard_map.59 = bf16[8,160,128]{2,1,0:T(8,128)(2,1)S(1)} custom-call(s32[3]{0:T(128)S(1)} %pad_add_fusion.refs_0_, f32[64,128]{1,0:T(8,128)S(1)} %bitcast.22, bf16[128,32,128]{2,1,0:T(8,128)(2,1)S(1)} %copy-done), custom_call_target="tpu_custom_call" | custom-call | flops 67108864 | bytes 2785292 | tf_op jit(solution)/shard_map/pallas_call | solution.py:103
  27.6 18.3 %all_to_all.42.refs_0_ = bf16[8,160,128]{2,1,0:T(8,128)(2,1)S(1)} all-to-all(bf16[8,160,128]{2,1,0:T(8,128)(2,1)S(1)} %shard_map.59), channel_id=1, replica_groups=mesh['ia'=4,'ja'=16,'ka'=8] {'ka'}, dimensions={0} | all-to-all | bytes 655360 | tf_op jit(solution)/shard_map/all_to_all | solution.py:329
  46.0 1.0 shard_map.60
  47.0 12.7 %all_to_all.43.refs_0_ = f32[16,8,128]{2,1,0:T(8,128)S(1)} all-to-all(f32[16,8,128]{2,1,0:T(8,128)S(1)} %get-tuple-element.21), channel_id=1, replica_groups=mesh['ia'=4,'ja'=16,'ka'=8] {'ja'}, dimensions={0} | all-to-all | bytes 131072 | tf_op jit(solution)/shard_map/all_to_all | solution.py:329
  59.8 0.3 shard_map.61
  60.1 12.9 %all_to_all.44 = f32[384,1,128]{2,1,0:T(1,128)S(1)} all-to-all(f32[384,1,128]{2,1,0:T(1,128)S(1)} %bitcast.21), channel_id=1, replica_groups=mesh['ia'=4,'ja'=16,'ka'=8] {'ia','ka'}, dimensions={0} | all-to-all | bytes 393216 | tf_op jit(solution)/shard_map/all_to_all | solution.py:329
  73.0 2.3 %shard_map.62 = (f32[16,24,128]{2,1,0:T(8,128)S(1)}, f32[32,32]{1,0:T(8,128)S(1)}, f32[128,32]{1,0:T(8,128)S(1)}, f32[32,32]{1,0:T(8,128)S(1)}) custom-call(s32[3]{0:T(128)S(1)} %pad_add_fusion.refs_0_, f32[384,128]{1,0:T(8,128)S(1)} %bitcast.20, f32[32,32]{1,0:T(8,128)S(1)} %get-tuple-element.24.refs_2_, bf16[32,128,128]{2,1,0:T(8,128)(2,1)S(1)} %bitcast.19), custom_call_target="tpu_custom_call" | custom-call | flops 67108864 | bytes 2519052 | tf_op jit(solution)/shard_map/pallas_call | solution.py:103
  75.3 14.8 %all_to_all.45.got_ref = f32[16,24,128]{2,1,0:T(8,128)S(1)} all-to-all(f32[16,24,128]{2,1,0:T(8,128)S(1)} %get-tuple-element.26), channel_id=1, replica_groups=mesh['ia'=4,'ja'=16,'ka'=8] {'ja'}, dimensions={0} | all-to-all | bytes 393216 | tf_op jit(solution)/shard_map/all_to_all | solution.py:329
  90.1 0.6 shard_map.63
  90.7 3.4 %all-to-all-start.5 = ((f32[8,16,128]{2,1,0:T(8,128)}), f32[8,16,128]{2,1,0:T(8,128)S(1)}, u32[]{:S(2)}, u32[]{:S(2)}) async-start(f32[8,16,128]{2,1,0:T(8,128)} %get-tuple-element.33), calls=%async_computation.5 | async-start | bytes 131072 | tf_op jit(solution)/shard_map/all_to_all | solution.py:329
  94.1 1.9 %shard_map.64 = (f32[32,32]{1,0:T(8,128)S(1)}, f32[1,32]{1,0:T(1,128)}, f32[1,32]{1,0:T(1,128)}) custom-call(s32[3]{0:T(128)S(1)} %pad_add_fusion.refs_0_, f32[8,128]{1,0:T(8,128)S(1)} %get-tuple-element.27.refs_1_, f32[32,32]{1,0:T(8,128)S(1)} %get-tuple-element.28.refs_2_, f32[128,32]{1,0:T(8,128)S(1)} %get-tuple-element.29.refs_3_, ...), custom_call_target="tpu_custom_call" | custom-call | flops 16777216 | bytes 33036 | tf_op jit(solution)/shard_map/pallas_call | solution.py:103
  96.1 2.9 %all-to-all-done.5.refs_1_ = f32[8,16,128]{2,1,0:T(8,128)S(1)} async-done(((f32[8,16,128]{2,1,0:T(8,128)}), f32[8,16,128]{2,1,0:T(8,128)S(1)}, u32[]{:S(2)}, u32[]{:S(2)}) %all-to-all-start.5) | async-done | bytes 65568 | tf_op jit(solution)/shard_map/all_to_all | solution.py:329
  99.0 0.8 shard_map.65
  99.8 9.2 %all_to_all.46.refs_0_ = f32[8,8,128]{2,1,0:T(8,128)S(1)} all-to-all(f32[8,8,128]{2,1,0:T(8,128)S(1)} %get-tuple-element.35), channel_id=1, replica_groups=mesh['ia'=4,'ja'=16,'ka'=8] {'ka'}, dimensions={0} | all-to-all | bytes 65536 | tf_op jit(solution)/shard_map/all_to_all | solution.py:329
  109.1 0.6 shard_map.66
Async XLA Ops:
  0.6 0.7 copy-start.1
  0.6 0.7 copy-start.2
  2.0 24.1 %all-to-all-start = ((f32[64,1,128]{2,1,0:T(1,128)}), f32[64,1,128]{2,1,0:T(1,128)S(1)}, u32[]{:S(2)}, u32[]{:S(2)}) async-start(f32[64,1,128]{2,1,0:T(1,128)} %bitcast.6), calls=%async_computation | async-start | bytes 65536 | tf_op jit(solution)/shard_map/all_to_all | solution.py:329
  16.8 9.3 %copy-start = (bf16[128,32,128]{2,1,0:T(8,128)(2,1)S(1)}, bf16[128,32,128]{2,1,0:T(8,128)(2,1)}, u32[]{:S(2)}) copy-start(bf16[128,32,128]{2,1,0:T(8,128)(2,1)} %refs_2_.1) | copy-start | bytes 3145732
  90.7 8.3 %all-to-all-start.5 = ((f32[8,16,128]{2,1,0:T(8,128)}), f32[8,16,128]{2,1,0:T(8,128)S(1)}, u32[]{:S(2)}, u32[]{:S(2)}) async-start(f32[8,16,128]{2,1,0:T(8,128)} %get-tuple-element.33), calls=%async_computation.5 | async-start | bytes 131072 | tf_op jit(solution)/shard_map/all_to_all | solution.py:329

commit v6 on v5

--- a/solution.py
+++ b/solution.py
@@ -195,10 +195,10 @@
     rows_j = block_b.shape[0]
     wide_b = jnp.concatenate([block_b] * PACK, axis=1)
     terms = along.reshape(low_i, rows_j, LANES) * wide_b[None]
-    summed = jnp.concatenate(
-        [jnp.sum(terms, axis=1), jnp.zeros((8 - low_i, LANES), F32)], axis=0
-    )
-    send_ref[...] = jnp.broadcast_to(summed[None], send_ref.shape)
+    summed = jnp.sum(terms, axis=1)
+    rows = jnp.concatenate([summed] * (SUB // low_i), axis=0)
+    for start in range(0, send_ref.shape[0], SUB):
+        send_ref[start : start + SUB, :] = rows
     first_weights(grams_ref, weights_ref, gram_ref)
 
 
@@ -218,8 +218,11 @@
 
 
 def second_kernel(low_i, got_ref, weights_ref, along_ref, send_ref):
-    summed = jnp.sum(got_ref[...], axis=0)
-    solved = dot(summed, weights_ref[...])[0:low_i]
+    wide = jnp.sum(got_ref[...].reshape(got_ref.shape[0] // SUB, SUB, LANES), axis=0)
+    summed = wide[0:low_i]
+    for start in range(low_i, SUB, low_i):
+        summed += wide[start : start + low_i]
+    solved = dot(summed, weights_ref[...])
     rows_j = along_ref.shape[0] // low_i
     terms = along_ref[...].reshape(low_i, rows_j, LANES) * solved[:, None, :]
     wide = jnp.sum(terms, axis=0)
@@ -313,7 +316,7 @@
     solved_ref[...] = solved
     squares = jnp.sum(solved * solved, axis=0, keepdims=True)
     squares = jnp.concatenate([squares, jnp.zeros((1, LANES - R), F32)], axis=1)
-    send_ref[...] = jnp.broadcast_to(squares[None], send_ref.shape)
+    send_ref[...] = jnp.broadcast_to(squares, send_ref.shape)
     own = 2 * (ia * n_ja + ja)
     own_c_ref[...] = jnp.concatenate(
         [solved_ref[pl.ds(own, 1), :], solved_ref[pl.ds(own + 1, 1), :]], axis=0
@@ -321,12 +324,16 @@
 
 
 def last_kernel(total, got_ref, own_c_ref, out_ref):
-    squares = jnp.sum(got_ref[...], axis=0)[0:1, 0:R]
+    squares = jnp.sum(got_ref[...], axis=0, keepdims=True)[:, 0:R]
     out_ref[...] = own_c_ref[...] * lax.rsqrt(squares / total + 1e-06)
 
 
 def exchange(blocks, axes, groups=None):
     return lax.all_to_all(blocks, axes, 0, 0, tiled=True, axis_index_groups=groups)
+
+
+def exchange_rows(rows, axes):
+    return exchange(rows[:, None, :], axes)[:, 0, :]
 
 
 def local(tensor, factor_b, factor_c):
@@ -355,19 +362,19 @@
     got = exchange(send, "ka")
     send, along, weights_a, gram_c = call(
         lambda *refs: first_kernel(low_i, *refs),
-        [shape(n_ja, 8, LANES), shape(low_i * rows_j, LANES), shape(LANES, LANES), shape(R, R)],
+        [shape(n_ja * low_i, LANES), shape(low_i * rows_j, LANES), shape(LANES, LANES), shape(R, R)],
         [got],
         2**20,
         scratch=[(2 * SUB, LANES)],
     )
-    got = exchange(send, "ja")
+    got = exchange_rows(send, "ja")
     (send,) = call(
         lambda *refs: second_kernel(low_i, *refs),
         [shape(n_ia * n_ka * (SUB + low_i), LANES)],
         [got, weights_a, along],
         2**20,
     )
-    got = exchange(send[:, None, :], ("ia", "ka"))[:, 0, :]
+    got = exchange_rows(send, ("ia", "ka"))
     send, gram_a, factor_a, solved_b = call(
         lambda *refs: third_kernel(totals, sizes, low_i, *refs),
         [
@@ -395,13 +402,13 @@
     )
     send, own_c = call(
         lambda *refs: fourth_kernel(sizes, *refs),
-        [shape(n_ka, 8, LANES), shape(2, R)],
+        [shape(n_ka, LANES), shape(2, R)],
         [place, got, weights_c],
         2**20,
         scalars=1,
         scratch=[(rows_k, R)],
     )
-    got = exchange(send, "ka")
+    got = exchange_rows(send, "ka")
     (out_c,) = call(
         lambda *refs: last_kernel(totals[2], *refs), [shape(2, R)], [got, own_c], 2**12
     )

time: 110 us -> 109 us (level)
  no operation moved by 1% of the time
where the time goes in v6:
time: 109 us
  blocking collectives  67.8 us (62%)
  starting transfers between devices  18.1 us (17%)
  waiting for transfers between devices  10 us (9%)
  Pallas kernels  9.81 us (9%)
  local copies, waits for them, and re-layouts  2.39 us (2%)
    all_to_all x5, blocking collectives, exchange(): lax.all_to_all(blocks, axes, 0, 0, tiled=True, axis_index_groups=groups)  67.8 us
    all_to_all x2, starting transfers between devices, exchange(): lax.all_to_all(blocks, axes, 0, 0, tiled=True, axis_index_groups=groups)  18.1 us
    all_to_all x2, waiting for transfers between devices, exchange(): lax.all_to_all(blocks, axes, 0, 0, tiled=True, axis_index_groups=groups)  10 us
    pallas_call x9, Pallas kernels, call(): pl.pallas_call(kernel, out_shape=outs, in_specs=spec, out_specs=[pl.Block...  9.81 us
    unnamed x7, local copies, waits for them, and re-layouts  2.39 us
  transfers between devices with their start and end apart: 2, of which 2 were waited for; matrix products, arithmetic and copies ran while one was open for 2% of the time, Pallas kernels for 2%

profile of v6, /device:TPU:1, one launch (start us, length us, event | category | flops | bytes accessed | tf_op | source)
XLA Modules:
  0.0 109.0 jit_solution(14200736155347600418)
XLA Ops:
  0.6 0.0 copy-start.1
  0.6 0.0 copy-start.2
  0.7 0.7 copy-done.1
  1.3 0.0 copy-done.2
  1.3 0.7 shard_map.58
  2.0 14.8 %all-to-all-start = ((f32[64,1,128]{2,1,0:T(1,128)}), f32[64,1,128]{2,1,0:T(1,128)S(1)}, u32[]{:S(2)}, u32[]{:S(2)}) async-start(f32[64,1,128]{2,1,0:T(1,128)} %bitcast.6), calls=%async_computation | async-start | bytes 65536 | tf_op jit(solution)/shard_map/all_to_all | solution.py:332
  16.8 0.0 copy-start
  16.8 1.7 %copy.13 = bf16[128,32,128]{2,0,1:T(8,128)(2,1)S(1)} copy(bf16[128,32,128]{2,1,0:T(8,128)(2,1)} %refs_2_.1) | data formatting | bytes 2097152 | tf_op args[0]
  18.6 0.1 pad_add_fusion.refs_0_
  18.7 7.5 %all-to-all-done = f32[64,1,128]{2,1,0:T(1,128)S(1)} async-done(((f32[64,1,128]{2,1,0:T(1,128)}), f32[64,1,128]{2,1,0:T(1,128)S(1)}, u32[]{:S(2)}, u32[]{:S(2)}) %all-to-all-start) | async-done | bytes 32800 | tf_op jit(solution)/shard_map/all_to_all | solution.py:332
  26.1 0.0 copy-done
  26.1 1.5 %shard_map.59 = bf16[8,160,128]{2,1,0:T(8,128)(2,1)S(1)} custom-call(s32[3]{0:T(128)S(1)} %pad_add_fusion.refs_0_, f32[64,128]{1,0:T(8,128)S(1)} %bitcast.30, bf16[128,32,128]{2,1,0:T(8,128)(2,1)S(1)} %copy-done), custom_call_target="tpu_custom_call" | custom-call | flops 67108864 | bytes 2785292 | tf_op jit(solution)/shard_map/pallas_call | solution.py:103
  27.6 18.3 %all_to_all.42.refs_0_ = bf16[8,160,128]{2,1,0:T(8,128)(2,1)S(1)} all-to-all(bf16[8,160,128]{2,1,0:T(8,128)(2,1)S(1)} %shard_map.59), channel_id=1, replica_groups=mesh['ia'=4,'ja'=16,'ka'=8] {'ka'}, dimensions={0} | all-to-all | bytes 655360 | tf_op jit(solution)/shard_map/all_to_all | solution.py:332
  46.0 1.0 shard_map.60
  47.0 12.4 %all_to_all.43 = f32[64,1,128]{2,1,0:T(1,128)S(1)} all-to-all(f32[64,1,128]{2,1,0:T(1,128)S(1)} %bitcast.32), channel_id=1, replica_groups=mesh['ia'=4,'ja'=16,'ka'=8] {'ja'}, dimensions={0} | all-to-all | bytes 65536 | tf_op jit(solution)/shard_map/all_to_all | solution.py:332
  59.4 0.3 shard_map.61
  59.7 12.4 %all_to_all.44 = f32[384,1,128]{2,1,0:T(1,128)S(1)} all-to-all(f32[384,1,128]{2,1,0:T(1,128)S(1)} %bitcast.29), channel_id=1, replica_groups=mesh['ia'=4,'ja'=16,'ka'=8] {'ia','ka'}, dimensions={0} | all-to-all | bytes 393216 | tf_op jit(solution)/shard_map/all_to_all | solution.py:332
  72.1 2.3 %shard_map.62 = (f32[16,24,128]{2,1,0:T(8,128)S(1)}, f32[32,32]{1,0:T(8,128)S(1)}, f32[128,32]{1,0:T(8,128)S(1)}, f32[32,32]{1,0:T(8,128)S(1)}) custom-call(s32[3]{0:T(128)S(1)} %pad_add_fusion.refs_0_, f32[384,128]{1,0:T(8,128)S(1)} %bitcast.28, f32[32,32]{1,0:T(8,128)S(1)} %get-tuple-element.24.refs_2_, bf16[32,128,128]{2,1,0:T(8,128)(2,1)S(1)} %bitcast.27), custom_call_target="tpu_custom_call" | custom-call | flops 67108864 | bytes 2519052 | tf_op jit(solution)/shard_map/pallas_call | solution.py:103
  74.4 15.8 %all_to_all.45.got_ref = f32[16,24,128]{2,1,0:T(8,128)S(1)} all-to-all(f32[16,24,128]{2,1,0:T(8,128)S(1)} %get-tuple-element.26), channel_id=1, replica_groups=mesh['ia'=4,'ja'=16,'ka'=8] {'ja'}, dimensions={0} | all-to-all | bytes 393216 | tf_op jit(solution)/shard_map/all_to_all | solution.py:332
  90.3 0.6 shard_map.63
  90.9 3.3 %all-to-all-start.5 = ((f32[8,16,128]{2,1,0:T(8,128)}), f32[8,16,128]{2,1,0:T(8,128)S(1)}, u32[]{:S(2)}, u32[]{:S(2)}) async-start(f32[8,16,128]{2,1,0:T(8,128)} %get-tuple-element.33), calls=%async_computation.5 | async-start | bytes 131072 | tf_op jit(solution)/shard_map/all_to_all | solution.py:332
  94.2 1.9 %shard_map.64 = (f32[32,32]{1,0:T(8,128)S(1)}, f32[1,32]{1,0:T(1,128)}, f32[1,32]{1,0:T(1,128)}) custom-call(s32[3]{0:T(128)S(1)} %pad_add_fusion.refs_0_, f32[8,128]{1,0:T(8,128)S(1)} %get-tuple-element.27.refs_1_, f32[32,32]{1,0:T(8,128)S(1)} %get-tuple-element.28.refs_2_, f32[128,32]{1,0:T(8,128)S(1)} %get-tuple-element.29.refs_3_, ...), custom_call_target="tpu_custom_call" | custom-call | flops 16777216 | bytes 33036 | tf_op jit(solution)/shard_map/pallas_call | solution.py:103
  96.1 2.6 %all-to-all-done.5.refs_1_ = f32[8,16,128]{2,1,0:T(8,128)S(1)} async-done(((f32[8,16,128]{2,1,0:T(8,128)}), f32[8,16,128]{2,1,0:T(8,128)S(1)}, u32[]{:S(2)}, u32[]{:S(2)}) %all-to-all-start.5) | async-done | bytes 65568 | tf_op jit(solution)/shard_map/all_to_all | solution.py:332
  98.7 0.8 shard_map.65
  99.5 8.9 %all_to_all.46 = f32[8,1,128]{2,1,0:T(1,128)S(1)} all-to-all(f32[8,1,128]{2,1,0:T(1,128)S(1)} %bitcast.34), channel_id=1, replica_groups=mesh['ia'=4,'ja'=16,'ka'=8] {'ka'}, dimensions={0} | all-to-all | bytes 8192 | tf_op jit(solution)/shard_map/all_to_all | solution.py:332
  108.4 0.6 shard_map.66
Async XLA Ops:
  0.6 0.7 copy-start.1
  0.6 0.7 copy-start.2
  2.0 24.1 %all-to-all-start = ((f32[64,1,128]{2,1,0:T(1,128)}), f32[64,1,128]{2,1,0:T(1,128)S(1)}, u32[]{:S(2)}, u32[]{:S(2)}) async-start(f32[64,1,128]{2,1,0:T(1,128)} %bitcast.6), calls=%async_computation | async-start | bytes 65536 | tf_op jit(solution)/shard_map/all_to_all | solution.py:332
  16.8 9.3 %copy-start = (bf16[128,32,128]{2,1,0:T(8,128)(2,1)S(1)}, bf16[128,32,128]{2,1,0:T(8,128)(2,1)}, u32[]{:S(2)}) copy-start(bf16[128,32,128]{2,1,0:T(8,128)(2,1)} %refs_2_.1) | copy-start | bytes 3145732
  90.9 7.8 %all-to-all-start.5 = ((f32[8,16,128]{2,1,0:T(8,128)}), f32[8,16,128]{2,1,0:T(8,128)S(1)}, u32[]{:S(2)}, u32[]{:S(2)}) async-start(f32[8,16,128]{2,1,0:T(8,128)} %get-tuple-element.33), calls=%async_computation.5 | async-start | bytes 131072 | tf_op jit(solution)/shard_map/all_to_all | solution.py:332

commit v7 on v6

--- a/solution.py
+++ b/solution.py
@@ -122,20 +122,16 @@
     send_ref[...] = jnp.broadcast_to(row, send_ref.shape)
 
 
-def along_kernel(sizes, place_ref, rows_ref, tensor_ref, send_ref):
+def along_kernel(sizes, place_ref, rows_ref, tensor_ref, send_ref, block_ref):
     n_ia, n_ja, n_ka = sizes
     rows_i, rows_j, rows_k = tensor_ref.shape
     ja = place_ref[1]
     rows = rows_ref[...]
     sources = rows.shape[0]
-    k_of = lax.broadcasted_iota(jnp.int32, (rows_k, sources), 0)
-    d_of = lax.broadcasted_iota(jnp.int32, (rows_k, sources), 1)
-    low = rows.astype(BF16)
-    even = jnp.where(k_of == 2 * d_of, 1.0, 0.0).astype(BF16)
-    odd = jnp.where(k_of == 2 * d_of + 1, 1.0, 0.0).astype(BF16)
-    block_c = jnp.dot(even, low[:, R : 2 * R], preferred_element_type=F32)
-    block_c += jnp.dot(odd, low[:, 2 * R : 3 * R], preferred_element_type=F32)
-    tiled = jnp.concatenate([block_c] * PACK, axis=1)
+    for t in range(2):
+        one = rows[:, (t + 1) * R : (t + 2) * R]
+        block_ref[pl.ds(t, sources, stride=2), :] = jnp.concatenate([one] * PACK, axis=1)
+    tiled = block_ref[0:rows_k, :]
     lane = lax.broadcasted_iota(jnp.int32, (rows_k, LANES), 1) // R
     weights = jnp.concatenate(
         [jnp.where(lane == g, tiled, 0.0).astype(BF16) for g in range(PACK)], axis=0
@@ -358,6 +354,7 @@
         [place, rows, tensor],
         2**26,
         scalars=1,
+        scratch=[(rows_k + 8, LANES)],
     )
     got = exchange(send, "ka")
     send, along, weights_a, gram_c = call(

time: 109 us -> 109 us (level)
  no operation moved by 1% of the time
where the time goes in v7:
time: 109 us
  blocking collectives  67.8 us (62%)
  starting transfers between devices  18.1 us (17%)
  waiting for transfers between devices  10 us (9%)
  Pallas kernels  9.63 us (9%)
  local copies, waits for them, and re-layouts  2.39 us (2%)
    all_to_all x5, blocking collectives, exchange(): lax.all_to_all(blocks, axes, 0, 0, tiled=True, axis_index_groups=groups)  67.8 us
    all_to_all x2, starting transfers between devices, exchange(): lax.all_to_all(blocks, axes, 0, 0, tiled=True, axis_index_groups=groups)  18.1 us
    all_to_all x2, waiting for transfers between devices, exchange(): lax.all_to_all(blocks, axes, 0, 0, tiled=True, axis_index_groups=groups)  10 us
    pallas_call x9, Pallas kernels, call(): pl.pallas_call(kernel, out_shape=outs, in_specs=spec, out_specs=[pl.Block...  9.63 us
    unnamed x7, local copies, waits for them, and re-layouts  2.39 us
  transfers between devices with their start and end apart: 2, of which 2 were waited for; matrix products, arithmetic and copies ran while one was open for 2% of the time, Pallas kernels for 2%

profile of v7, /device:TPU:1, one launch (start us, length us, event | category | flops | bytes accessed | tf_op | source)
XLA Modules:
  0.0 108.8 jit_solution(17789616650998078548)
XLA Ops:
  0.6 0.0 copy-start.1
  0.6 0.0 copy-start.2
  0.7 0.7 copy-done.1
  1.3 0.0 copy-done.2
  1.3 0.7 shard_map.58
  2.0 14.8 %all-to-all-start = ((f32[64,1,128]{2,1,0:T(1,128)}), f32[64,1,128]{2,1,0:T(1,128)S(1)}, u32[]{:S(2)}, u32[]{:S(2)}) async-start(f32[64,1,128]{2,1,0:T(1,128)} %bitcast.6), calls=%async_computation | async-start | bytes 65536 | tf_op jit(solution)/shard_map/all_to_all | solution.py:328
  16.8 0.0 copy-start
  16.8 1.7 %copy.13 = bf16[128,32,128]{2,0,1:T(8,128)(2,1)S(1)} copy(bf16[128,32,128]{2,1,0:T(8,128)(2,1)} %refs_2_.1) | data formatting | bytes 2097152 | tf_op args[0]
  18.6 0.1 pad_add_fusion.refs_0_
  18.7 7.5 %all-to-all-done = f32[64,1,128]{2,1,0:T(1,128)S(1)} async-done(((f32[64,1,128]{2,1,0:T(1,128)}), f32[64,1,128]{2,1,0:T(1,128)S(1)}, u32[]{:S(2)}, u32[]{:S(2)}) %all-to-all-start) | async-done | bytes 32800 | tf_op jit(solution)/shard_map/all_to_all | solution.py:328
  26.1 0.0 copy-done
  26.1 1.3 %shard_map.59 = bf16[8,160,128]{2,1,0:T(8,128)(2,1)S(1)} custom-call(s32[3]{0:T(128)S(1)} %pad_add_fusion.refs_0_, f32[64,128]{1,0:T(8,128)S(1)} %bitcast.30, bf16[128,32,128]{2,1,0:T(8,128)(2,1)S(1)} %copy-done), custom_call_target="tpu_custom_call" | custom-call | flops 67108864 | bytes 2785292 | tf_op jit(solution)/shard_map/pallas_call | solution.py:103
  27.5 18.3 %all_to_all.42.refs_0_ = bf16[8,160,128]{2,1,0:T(8,128)(2,1)S(1)} all-to-all(bf16[8,160,128]{2,1,0:T(8,128)(2,1)S(1)} %shard_map.59), channel_id=1, replica_groups=mesh['ia'=4,'ja'=16,'ka'=8] {'ka'}, dimensions={0} | all-to-all | bytes 655360 | tf_op jit(solution)/shard_map/all_to_all | solution.py:328
  45.8 1.0 shard_map.60
  46.8 12.4 %all_to_all.43 = f32[64,1,128]{2,1,0:T(1,128)S(1)} all-to-all(f32[64,1,128]{2,1,0:T(1,128)S(1)} %bitcast.32), channel_id=1, replica_groups=mesh['ia'=4,'ja'=16,'ka'=8] {'ja'}, dimensions={0} | all-to-all | bytes 65536 | tf_op jit(solution)/shard_map/all_to_all | solution.py:328
  59.2 0.3 shard_map.61
  59.5 12.4 %all_to_all.44 = f32[384,1,128]{2,1,0:T(1,128)S(1)} all-to-all(f32[384,1,128]{2,1,0:T(1,128)S(1)} %bitcast.29), channel_id=1, replica_groups=mesh['ia'=4,'ja'=16,'ka'=8] {'ia','ka'}, dimensions={0} | all-to-all | bytes 393216 | tf_op jit(solution)/shard_map/all_to_all | solution.py:328
  71.9 2.3 %shard_map.62 = (f32[16,24,128]{2,1,0:T(8,128)S(1)}, f32[32,32]{1,0:T(8,128)S(1)}, f32[128,32]{1,0:T(8,128)S(1)}, f32[32,32]{1,0:T(8,128)S(1)}) custom-call(s32[3]{0:T(128)S(1)} %pad_add_fusion.refs_0_, f32[384,128]{1,0:T(8,128)S(1)} %bitcast.28, f32[32,32]{1,0:T(8,128)S(1)} %get-tuple-element.24.refs_2_, bf16[32,128,128]{2,1,0:T(8,128)(2,1)S(1)} %bitcast.27), custom_call_target="tpu_custom_call" | custom-call | flops 67108864 | bytes 2519052 | tf_op jit(solution)/shard_map/pallas_call | solution.py:103
  74.2 15.8 %all_to_all.45.got_ref = f32[16,24,128]{2,1,0:T(8,128)S(1)} all-to-all(f32[16,24,128]{2,1,0:T(8,128)S(1)} %get-tuple-element.26), channel_id=1, replica_groups=mesh['ia'=4,'ja'=16,'ka'=8] {'ja'}, dimensions={0} | all-to-all | bytes 393216 | tf_op jit(solution)/shard_map/all_to_all | solution.py:328
  90.1 0.6 shard_map.63
  90.7 3.3 %all-to-all-start.5 = ((f32[8,16,128]{2,1,0:T(8,128)}), f32[8,16,128]{2,1,0:T(8,128)S(1)}, u32[]{:S(2)}, u32[]{:S(2)}) async-start(f32[8,16,128]{2,1,0:T(8,128)} %get-tuple-element.33), calls=%async_computation.5 | async-start | bytes 131072 | tf_op jit(solution)/shard_map/all_to_all | solution.py:328
  94.0 1.9 %shard_map.64 = (f32[32,32]{1,0:T(8,128)S(1)}, f32[1,32]{1,0:T(1,128)}, f32[1,32]{1,0:T(1,128)}) custom-call(s32[3]{0:T(128)S(1)} %pad_add_fusion.refs_0_, f32[8,128]{1,0:T(8,128)S(1)} %get-tuple-element.27.refs_1_, f32[32,32]{1,0:T(8,128)S(1)} %get-tuple-element.28.refs_2_, f32[128,32]{1,0:T(8,128)S(1)} %get-tuple-element.29.refs_3_, ...), custom_call_target="tpu_custom_call" | custom-call | flops 16777216 | bytes 33036 | tf_op jit(solution)/shard_map/pallas_call | solution.py:103
  96.0 2.6 %all-to-all-done.5.refs_1_ = f32[8,16,128]{2,1,0:T(8,128)S(1)} async-done(((f32[8,16,128]{2,1,0:T(8,128)}), f32[8,16,128]{2,1,0:T(8,128)S(1)}, u32[]{:S(2)}, u32[]{:S(2)}) %all-to-all-start.5) | async-done | bytes 65568 | tf_op jit(solution)/shard_map/all_to_all | solution.py:328
  98.5 0.8 shard_map.65
  99.3 8.9 %all_to_all.46 = f32[8,1,128]{2,1,0:T(1,128)S(1)} all-to-all(f32[8,1,128]{2,1,0:T(1,128)S(1)} %bitcast.34), channel_id=1, replica_groups=mesh['ia'=4,'ja'=16,'ka'=8] {'ka'}, dimensions={0} | all-to-all | bytes 8192 | tf_op jit(solution)/shard_map/all_to_all | solution.py:328
  108.2 0.6 shard_map.66
Async XLA Ops:
  0.6 0.7 copy-start.1
  0.6 0.7 copy-start.2
  2.0 24.1 %all-to-all-start = ((f32[64,1,128]{2,1,0:T(1,128)}), f32[64,1,128]{2,1,0:T(1,128)S(1)}, u32[]{:S(2)}, u32[]{:S(2)}) async-start(f32[64,1,128]{2,1,0:T(1,128)} %bitcast.6), calls=%async_computation | async-start | bytes 65536 | tf_op jit(solution)/shard_map/all_to_all | solution.py:328
  16.8 9.3 %copy-start = (bf16[128,32,128]{2,1,0:T(8,128)(2,1)S(1)}, bf16[128,32,128]{2,1,0:T(8,128)(2,1)}, u32[]{:S(2)}) copy-start(bf16[128,32,128]{2,1,0:T(8,128)(2,1)} %refs_2_.1) | copy-start | bytes 3145732
  90.7 7.8 %all-to-all-start.5 = ((f32[8,16,128]{2,1,0:T(8,128)}), f32[8,16,128]{2,1,0:T(8,128)S(1)}, u32[]{:S(2)}, u32[]{:S(2)}) async-start(f32[8,16,128]{2,1,0:T(8,128)} %get-tuple-element.33), calls=%async_computation.5 | async-start | bytes 131072 | tf_op jit(solution)/shard_map/all_to_all | solution.py:328
